TPU v7x, 768 devices: a whole 4x8x12 slice. The times are simulated.
768 devices in a mesh: lat: 64 (over x, z_hi, y), lon: 12 (over z_lo, core).
Axes of the slice: x: 4, y: 8, z: 12 (z_hi: 2, z_lo: 6; z = z_hi * 6 + z_lo), core: 2. Of those that a mesh axis runs over, the one named last changes fastest.
Arguments:
- tracers: float32 [5, 16, 576, 1440], P(None, None, 'lat', 'lon'), may hold values from -6 to 6
- zonal_wind: float32 [16, 576, 1440], P(None, 'lat', 'lon'), may hold values from -0.45 to 0.45
- meridional_wind: float32 [16, 576, 1440], P(None, 'lat', 'lon'), may hold values from -0.45 to 0.45
- cutoff: int32 [576], P('lat'), may hold values from 1 to 720, as said below
Outputs:
- filtered: float32 [5, 16, 576, 1440], P(None, None, 'lat', 'lon')
Inputs may be any that keep to these rules, and one draw needn't show every extreme that they name: cutoff is 720 on every row at least 96 rows from both poles and below it on the rows nearer a pole; it is 1 on row 0 and row 575.
All inputs are finite; a program needn't handle non-finite values.
Results may differ from a plain program's by a relative error of at most 0.000075.
Values sent between devices are 32-bit elements; how exact they have to be, the bound alone decides.
A program may use at most 32 MiB of HBM per device.

v0:
```python
import math

import jax
import jax.numpy as jnp
from jax import lax
from jax.sharding import PartitionSpec as P


def extended(block, sides, width):
    for axis, dim in sides:
        count = lax.axis_size(axis)
        forward = [(i, i + 1) for i in range(count - 1)]
        forward.append((count - 1, 0))
        backward = [(target, source) for source, target in forward]
        low = lax.ppermute(
            lax.slice_in_dim(block, block.shape[dim] - width, None, axis=dim), axis, forward
        )
        high = lax.ppermute(lax.slice_in_dim(block, 0, width, axis=dim), axis, backward)
        block = jnp.concatenate([low, block, high], axis=dim)
    return block


def from_behind(x, axis, by):
    count = lax.axis_size(axis)
    return lax.ppermute(x, axis, [(i, (i + by) % count) for i in range(count)])


def advect(q_pad, u_pad, v_pad):
    center = q_pad[..., 1:-1, 1:-1]
    u_mid = u_pad[..., 1:-1, 1:-1]
    east_speed = 0.5 * (u_mid + u_pad[..., 1:-1, 2:])
    west_speed = 0.5 * (u_pad[..., 1:-1, :-2] + u_mid)
    east_flux = (
        jnp.maximum(east_speed, 0.0) * center + jnp.minimum(east_speed, 0.0) * q_pad[..., 1:-1, 2:]
    )
    west_flux = (
        jnp.maximum(west_speed, 0.0) * q_pad[..., 1:-1, :-2] + jnp.minimum(west_speed, 0.0) * center
    )
    v_mid = v_pad[..., 1:-1, 1:-1]
    south_speed = 0.5 * (v_mid + v_pad[..., 2:, 1:-1])
    north_speed = 0.5 * (v_pad[..., :-2, 1:-1] + v_mid)
    south_flux = (
        jnp.maximum(south_speed, 0.0) * center
        + jnp.minimum(south_speed, 0.0) * q_pad[..., 2:, 1:-1]
    )
    north_flux = (
        jnp.maximum(north_speed, 0.0) * q_pad[..., :-2, 1:-1]
        + jnp.minimum(north_speed, 0.0) * center
    )
    return center - (east_flux - west_flux) - (south_flux - north_flux)


def table_rows(count, circle):
    lon_index = jnp.arange(count, dtype=jnp.int32)
    wave_number = jnp.arange(circle // 2 + 1, dtype=jnp.int32)
    phase = (lon_index[:, None] * wave_number[None, :] % circle).astype(jnp.float32) * (
        2.0 * math.pi / circle
    )
    return jnp.concatenate([jnp.cos(phase), jnp.sin(phase)], axis=1)


def spectral_scale(cut_rows, circle):
    half_lon = circle // 2
    wave_number = jnp.arange(half_lon + 1, dtype=jnp.int32)
    keep = (wave_number[None, :] <= cut_rows[:, None]).astype(jnp.float32)
    weight = jnp.where((wave_number == 0) | (wave_number == half_lon), 1.0, 2.0) / circle
    scaled = keep * weight[None, :]
    return jnp.concatenate([scaled, scaled], axis=1)


def inverse_rows(scaled, table):
    return lax.dot_general(
        scaled,
        table,
        (((1,), (1,)), ((), ())),
        precision=lax.Precision.HIGHEST,
        preferred_element_type=jnp.float32,
    )


def filter_circles(piece, cut_rows, circle):
    table = table_rows(circle, circle)
    coeffs = jnp.dot(
        piece, table, precision=lax.Precision.HIGHEST, preferred_element_type=jnp.float32
    )
    scaled = coeffs * spectral_scale(cut_rows, circle)
    return inverse_rows(scaled, table)


def body(tracers, zonal_wind, meridional_wind, cutoff):
    num_fields, num_levels, row_count, sector = tracers.shape
    field_planes = num_fields * num_levels
    planes = jnp.concatenate(
        [tracers.reshape(field_planes, row_count, sector), zonal_wind, meridional_wind], axis=0
    )
    padded = extended(planes, (("lat", 1), ("lon", 2)), 1)
    edges = jnp.stack([planes[:, 0, :], planes[:, -1, :]], axis=0)
    across = from_behind(edges, "lon", lax.axis_size("lon") // 2)
    flip = jnp.concatenate(
        [jnp.ones((field_planes + num_levels,), jnp.float32), -jnp.ones((num_levels,), jnp.float32)]
    )
    across = across * flip[None, :, None]
    lat_index = lax.axis_index("lat")
    top_row = jnp.where(lat_index == 0, across[0], padded[:, 0, 1:-1])
    bottom_row = jnp.where(lat_index == lax.axis_size("lat") - 1, across[1], padded[:, -1, 1:-1])
    padded = padded.at[:, 0, 1:-1].set(top_row).at[:, -1, 1:-1].set(bottom_row)
    q_pad = padded[:field_planes].reshape(num_fields, num_levels, row_count + 2, sector + 2)
    u_pad = padded[field_planes : field_planes + num_levels]
    v_pad = padded[field_planes + num_levels :]
    stepped = advect(q_pad, u_pad, v_pad)
    flat = stepped.reshape(field_planes * row_count, sector)
    n_sectors = lax.axis_size("lon")
    circle = sector * n_sectors
    polar = jnp.any(cutoff < circle // 2)
    cut_all = jnp.tile(cutoff, field_planes)
    lon_index = lax.axis_index("lon")
    share = lax.all_to_all(flat, "lon", split_axis=0, concat_axis=1, tiled=True)
    share_rows = share.shape[0]
    cut_rows = lax.dynamic_slice_in_dim(cut_all, lon_index * share_rows, share_rows, 0)
    done = lax.cond(polar, lambda: filter_circles(share, cut_rows, circle), lambda: share)
    result = lax.all_to_all(done, "lon", split_axis=1, concat_axis=0, tiled=True)
    return result.reshape(num_fields, num_levels, row_count, sector)


def solution(mesh):
    in_specs = (P(None, None, "lat", "lon"), P(None, "lat", "lon"), P(None, "lat", "lon"), P("lat"))
    out_specs = P(None, None, "lat", "lon")
    return jax.shard_map(body, mesh=mesh, in_specs=in_specs, out_specs=out_specs, check_vma=False)
```

profile of v0, /device:TPU:57, one launch (start us, length us, event | category | flops | bytes accessed | tf_op | source)
XLA Modules:
  0.0 133.8 jit_solution(10395928570673773169)
XLA Ops:
  0.0 1.0 copy.28
  1.1 0.8 pad_maximum_fusion.12
  1.8 14.1 %collective-permute-start = (f32[112,1,120]{2,0,1:T(8,128)S(1)}, f32[112,1,120]{2,0,1:T(8,128)S(1)}, u32[]{:S(2)}, u32[]{:S(2)}) collective-permute-start(f32[112,1,120]{2,0,1:T(8,128)S(1)} %get-tuple-element.76), channel_id=1, source_target_pairs={{0,12},{12,24},{24,36},{36,48},{48,60},{60,72},{72,84},{84,96},{96... | collective-permute-start | bytes 161288 | tf_op jit(solution)/shard_map/ppermute | solution.py:15
  15.9 1.9 %collective-permute-start.1 = (f32[112,1,120]{2,0,1:T(8,128)S(1)}, f32[112,1,120]{2,0,1:T(8,128)S(1)}, u32[]{:S(2)}, u32[]{:S(2)}) collective-permute-start(f32[112,1,120]{2,0,1:T(8,128)S(1)} %get-tuple-element.77), channel_id=1, source_target_pairs={{12,0},{24,12},{36,24},{48,36},{60,48},{72,60},{84,72},{96,84},{10... | collective-permute-start | bytes 161288 | tf_op jit(solution)/shard_map/ppermute | solution.py:18
  17.9 4.9 %collective-permute-start.4 = (f32[2,112,120]{2,1,0:T(8,128)S(1)}, f32[2,112,120]{2,1,0:T(8,128)S(1)}, u32[]{:S(2)}, u32[]{:S(2)}) collective-permute-start(f32[2,112,120]{2,1,0:T(8,128)S(1)} %pad_maximum_fusion.9), channel_id=1, source_target_pairs={{0,6},{1,7},{2,8},{3,9},{4,10},{5,11},{6,0},{7,1},{8,2},{9,3},{10,... | collective-permute-start | bytes 322568 | tf_op jit(solution)/shard_map/ppermute | solution.py:25
  22.8 6.6 %collective-permute-done.1 = f32[112,1,120]{2,0,1:T(8,128)S(1)} collective-permute-done((f32[112,1,120]{2,0,1:T(8,128)S(1)}, f32[112,1,120]{2,0,1:T(8,128)S(1)}, u32[]{:S(2)}, u32[]{:S(2)}) %collective-permute-start.1) | collective-permute-done | bytes 53792 | tf_op jit(solution)/shard_map/ppermute | solution.py:18
  29.4 1.0 pad_maximum_fusion.7
  30.3 0.2 fusion.28
  30.8 0.2 copy.30
  31.0 3.9 %collective-permute-start.3 = (f32[112,11,1]{0,2,1:T(1,128)S(1)}, f32[112,11,1]{0,2,1:T(1,128)S(1)}, u32[]{:S(2)}, u32[]{:S(2)}) collective-permute-start(f32[112,11,1]{0,2,1:T(1,128)S(1)} %copy.30), channel_id=1, source_target_pairs={{1,0},{2,1},{3,2},{4,3},{5,4},{6,5},{7,6},{8,7},{9,8},{10,9},{11,1... | collective-permute-start | bytes 14792 | tf_op jit(solution)/shard_map/ppermute | solution.py:18
  35.0 3.8 %collective-permute-start.2 = (f32[112,11,1]{0,2,1:T(1,128)S(1)}, f32[112,11,1]{0,2,1:T(1,128)S(1)}, u32[]{:S(2)}, u32[]{:S(2)}) collective-permute-start(f32[112,11,1]{0,2,1:T(1,128)S(1)} %copy.29), channel_id=1, source_target_pairs={{0,1},{1,2},{2,3},{3,4},{4,5},{5,6},{6,7},{7,8},{8,9},{9,10},{10,1... | collective-permute-start | bytes 14792 | tf_op jit(solution)/shard_map/ppermute | solution.py:15
  38.7 0.6 fusion.30
  39.3 3.1 %collective-permute-done.2 = f32[112,11,1]{0,2,1:T(1,128)S(1)} collective-permute-done((f32[112,11,1]{0,2,1:T(1,128)S(1)}, f32[112,11,1]{0,2,1:T(1,128)S(1)}, u32[]{:S(2)}, u32[]{:S(2)}) %collective-permute-start.2) | collective-permute-done | bytes 4960 | tf_op jit(solution)/shard_map/ppermute | solution.py:15
  42.5 0.3 copy.31
  42.7 0.3 copy.32
  43.0 0.4 pad_maximum_fusion.8
  43.6 1.7 %scatter.6 = f32[112,11,122]{2,0,1:T(8,128)S(1)} dynamic-update-slice(f32[112,11,122]{2,0,1:T(8,128)S(1)} %pad_maximum_fusion.8, f32[112,1,120]{2,0,1:T(8,128)S(1)} %get-tuple-element.84, s32[]{:T(128)} %constant.115.clone.1, s32[]{:T(128)} %bitcast.5, s32[]{:T(128)} %bitcast.6) | dynamic-update-slice | bytes 107524 | tf_op jit(solution)/shard_map/scatter | solution.py:106
  45.3 0.6 scatter.9
  46.4 0.4 fusion.29
  46.8 0.9 fusion.18
  47.8 0.8 all_to_all.29
  48.6 10.6 %all-to-all-start = ((f32[12,60,120]{2,1,0:T(8,128)}), f32[12,60,120]{2,1,0:T(8,128)S(1)}, u32[]{:S(2)}, u32[]{:S(2)}) async-start(f32[12,60,120]{2,1,0:T(8,128)} %all_to_all.29), calls=%async_computation | async-start | bytes 786432 | tf_op jit(solution)/shard_map/all_to_all | solution.py:117
  59.2 0.6 compare_reduce_fusion
  60.5 16.1 %all-to-all-done = f32[12,60,120]{2,1,0:T(8,128)S(1)} async-done(((f32[12,60,120]{2,1,0:T(8,128)}), f32[12,60,120]{2,1,0:T(8,128)S(1)}, u32[]{:S(2)}, u32[]{:S(2)}) %all-to-all-start) | async-done | bytes 345632 | tf_op jit(solution)/shard_map/all_to_all | solution.py:117
  76.6 0.2 copy.46
  77.0 33.3 %conditional.1 = (f32[60,1440]{1,0:T(8,128)S(1)}) conditional(s32[]{:T(128)} %convert_element_type.10, f32[60,1440]{1,0:T(8,128)S(1)} %all_to_all.32, (f32[60,1440]{1,0:T(8,128)S(1)}, s32[9]{0:T(128)S(1)}, s32[]{:T(128)}) %tuple.42), branch_computations={%region_1.2_spmd, %region_2.3_spmd} | conditional | flops 3003891200 | bytes 26662422 | solution.py:120
  77.5 18.4 %fusion.6 = (f32[1440,721]{1,0:T(8,128)S(1)}, f32[1440,721]{1,0:T(8,128)S(1)}) fusion(), kind=kLoop, calls=%fused_computation.9 | loop fusion | flops 9344160 | bytes 8305920 | tf_op jit(solution)/shard_map/cond/branch_1_fun/sin | solution.py:59
  96.0 6.1 %fusion.10 = f32[60,1442]{1,0:T(8,128)S(1)} fusion(f32[60,1440]{1,0:T(8,128)S(1)} %get-tuple-element.61, f32[1440,721]{1,0:T(8,128)S(1)} %get-tuple-element.64, f32[1440,721]{1,0:T(8,128)S(1)} %get-tuple-element.65, f32[60,721]{1,0:T(8,128)S(1)} %fusion.11), kind=kOutput, calls=%fused_computation.13 | convolution fusion | flops 1497315072 | bytes 9170640 | tf_op jit(solution)/shard_map/cond/branch_1_fun/dot_general | solution.py:83
  102.1 7.9 %fusion = f32[60,1440]{1,0:T(8,128)S(1)} fusion(f32[60,1442]{1,0:T(8,128)S(1)} %fusion.10, f32[1440,721]{1,0:T(8,128)S(1)} %get-tuple-element.64, f32[1440,721]{1,0:T(8,128)S(1)} %get-tuple-element.65), kind=kOutput, calls=%fused_computation.1 | convolution fusion | flops 1497142016 | bytes 8997600 | tf_op jit(solution)/shard_map/cond/branch_1_fun/dot_general | solution.py:72
  110.3 0.4 all_to_all.33
  110.9 22.1 %all_to_all.38 = f32[60,12,120]{2,0,1:T(8,128)S(1)} all-to-all(f32[60,12,120]{2,0,1:T(8,128)S(1)} %copy.47), channel_id=1, replica_groups=mesh['lat'=64,'lon'=12] {'lon'}, dimensions={1} | all-to-all | bytes 691200 | tf_op jit(solution)/shard_map/all_to_all | solution.py:121
  133.0 0.9 copy.48
  (34 shorter events, 1.5 us)
Async XLA Ops:
  0.0 43.0 %copy-start = (f32[16,9,120]{2,0,1:T(8,128)S(1)}, f32[16,9,120]{2,0,1:T(8,128)}, u32[]{:S(2)}) copy-start(f32[16,9,120]{2,0,1:T(8,128)} %param.12) | copy-start | bytes 207364
  0.0 43.0 %copy-start.1 = (f32[16,9,120]{2,0,1:T(8,128)S(1)}, f32[16,9,120]{2,0,1:T(8,128)}, u32[]{:S(2)}) copy-start(f32[16,9,120]{2,0,1:T(8,128)} %param.11) | copy-start | bytes 207364
  1.8 21.0 %collective-permute-start = (f32[112,1,120]{2,0,1:T(8,128)S(1)}, f32[112,1,120]{2,0,1:T(8,128)S(1)}, u32[]{:S(2)}, u32[]{:S(2)}) collective-permute-start(f32[112,1,120]{2,0,1:T(8,128)S(1)} %get-tuple-element.76), channel_id=1, source_target_pairs={{0,12},{12,24},{24,36},{36,48},{48,60},{60,72},{72,84},{84,96},{96... | collective-permute-start | bytes 161288 | tf_op jit(solution)/shard_map/ppermute | solution.py:15
  15.9 13.5 %collective-permute-start.1 = (f32[112,1,120]{2,0,1:T(8,128)S(1)}, f32[112,1,120]{2,0,1:T(8,128)S(1)}, u32[]{:S(2)}, u32[]{:S(2)}) collective-permute-start(f32[112,1,120]{2,0,1:T(8,128)S(1)} %get-tuple-element.77), channel_id=1, source_target_pairs={{12,0},{24,12},{36,24},{48,36},{60,48},{72,60},{84,72},{96,84},{10... | collective-permute-start | bytes 161288 | tf_op jit(solution)/shard_map/ppermute | solution.py:18
  17.8 25.6 %copy-start.2 = (f32[112]{0:T(128)S(1)}, f32[112]{0:T(128)}, u32[]{:S(2)}) copy-start(f32[112]{0:T(128)} %constant.116.clone.1) | copy-start | bytes 1348
  17.9 25.6 %collective-permute-start.4 = (f32[2,112,120]{2,1,0:T(8,128)S(1)}, f32[2,112,120]{2,1,0:T(8,128)S(1)}, u32[]{:S(2)}, u32[]{:S(2)}) collective-permute-start(f32[2,112,120]{2,1,0:T(8,128)S(1)} %pad_maximum_fusion.9), channel_id=1, source_target_pairs={{0,6},{1,7},{2,8},{3,9},{4,10},{5,11},{6,0},{7,1},{8,2},{9,3},{10,... | collective-permute-start | bytes 322568 | tf_op jit(solution)/shard_map/ppermute | solution.py:25
  31.0 11.7 %collective-permute-start.3 = (f32[112,11,1]{0,2,1:T(1,128)S(1)}, f32[112,11,1]{0,2,1:T(1,128)S(1)}, u32[]{:S(2)}, u32[]{:S(2)}) collective-permute-start(f32[112,11,1]{0,2,1:T(1,128)S(1)} %copy.30), channel_id=1, source_target_pairs={{1,0},{2,1},{3,2},{4,3},{5,4},{6,5},{7,6},{8,7},{9,8},{10,9},{11,1... | collective-permute-start | bytes 14792 | tf_op jit(solution)/shard_map/ppermute | solution.py:18
  35.0 7.5 %collective-permute-start.2 = (f32[112,11,1]{0,2,1:T(1,128)S(1)}, f32[112,11,1]{0,2,1:T(1,128)S(1)}, u32[]{:S(2)}, u32[]{:S(2)}) collective-permute-start(f32[112,11,1]{0,2,1:T(1,128)S(1)} %copy.29), channel_id=1, source_target_pairs={{0,1},{1,2},{2,3},{3,4},{4,5},{5,6},{6,7},{7,8},{8,9},{9,10},{10,1... | collective-permute-start | bytes 14792 | tf_op jit(solution)/shard_map/ppermute | solution.py:15
  46.4 12.8 %copy-start.3 = (s32[9]{0:T(128)S(1)}, s32[9]{0:T(128)}, u32[]{:S(2)}) copy-start(s32[9]{0:T(128)} %param.13) | copy-start | bytes 112
  48.6 28.0 %all-to-all-start = ((f32[12,60,120]{2,1,0:T(8,128)}), f32[12,60,120]{2,1,0:T(8,128)S(1)}, u32[]{:S(2)}, u32[]{:S(2)}) async-start(f32[12,60,120]{2,1,0:T(8,128)} %all_to_all.29), calls=%async_computation | async-start | bytes 786432 | tf_op jit(solution)/shard_map/all_to_all | solution.py:117
where the time goes:
time: 134 us
  starting transfers between devices  39.2 us (29%)
  waiting for transfers between devices  25.8 us (19%)
  other arithmetic  22.5 us (17%)
  blocking collectives  22.1 us (16%)
  matrix products  14.1 us (11%)
  local copies, waits for them, and re-layouts  8.74 us (7%)
    all_to_all x1, blocking collectives, body(): lax.all_to_all(done, 'lon', split_axis=1, concat_axis=0, tiled=True)  22.1 us
    sin x1, other arithmetic, table_rows(): return jnp.concatenate([jnp.cos(phase), jnp.sin(phase)], axis=1)  18.4 us
    ppermute x2, starting transfers between devices, extended(): lax.ppermute(lax.slice_in_dim(block, block.shape[dim] - width, None, axis...  17.8 us
    all_to_all x1, waiting for transfers between devices, body(): share = lax.all_to_all(flat, 'lon', split_axis=0, concat_axis=1, tiled=True)  16.1 us
    all_to_all x1, starting transfers between devices, body(): share = lax.all_to_all(flat, 'lon', split_axis=0, concat_axis=1, tiled=True)  10.6 us
    dot_general x1, matrix products, inverse_rows(): lax.dot_general(scaled, table, (((1,), (1,)), ((), ())), precision=lax.Pr...  7.94 us
    ppermute x2, waiting for transfers between devices, extended(): lax.ppermute(lax.slice_in_dim(block, 0, width, axis=dim), axis, backward)  6.57 us
    dot_general x1, matrix products, filter_circles(): jnp.dot(piece, table, precision=lax.Precision.HIGHEST, preferred_element_...  6.13 us
  transfers between devices with their start and end apart: 6, of which 3 were waited for; matrix products, arithmetic and copies ran while one was open for 3% of the time, Pallas kernels for 0%

commit v1 on v0

v1 whole, which is shorter than its diff:
```python
import functools
import math

import jax
import jax.numpy as jnp
import ml_dtypes
import numpy as np
from jax import lax
from jax.experimental import pallas as pl
from jax.experimental.pallas import tpu as pltpu
from jax.sharding import PartitionSpec as P

MESH = pl.DeviceIdType.MESH
POLAR_ROWS = 96
SECTORS = 12
LANES = 128


def split_bf16(table):
    high = table.astype(ml_dtypes.bfloat16)
    low = (table - high.astype(np.float64)).astype(ml_dtypes.bfloat16)
    return high, low


@functools.lru_cache(maxsize=None)
def dft_tables(circle, sector):
    forward = np.zeros((6, 256, 256))
    inverse = np.zeros((6, 256, 256))
    waves = np.zeros((8, 256))
    m = np.arange(sector)

    def put(block, column, k, part, weight, real_half):
        phase = 2.0 * math.pi * ((m * k) % circle) / circle
        cos, sin = np.cos(phase), np.sin(phase)
        waves[block, column] = min(k, circle - k)
        if real_half is not None:
            base = 128 * real_half
            row = cos if part == 0 else -sin
            forward[block, base : base + sector, column] = row
            inverse[block, column, base : base + sector] = weight * row / circle
            return
        if part == 0:
            forward[block, :sector, column] = cos
            forward[block, 128 : 128 + sector, column] = sin
            inverse[block, column, :sector] = weight * cos / circle
            inverse[block, column, 128 : 128 + sector] = weight * sin / circle
        else:
            forward[block, :sector, column] = -sin
            forward[block, 128 : 128 + sector, column] = cos
            inverse[block, column, :sector] = -weight * sin / circle
            inverse[block, column, 128 : 128 + sector] = weight * cos / circle

    half = sector // 2
    for q in range(half + 1):
        put(0, q, SECTORS * q, 0, 1.0 if q in (0, half) else 2.0, 0)
    for q in range(1, half):
        put(0, half + q, SECTORS * q, 1, 2.0, 0)
    for q in range(half):
        put(0, 128 + q, 6 + SECTORS * q, 0, 2.0, 1)
        put(0, 128 + half + q, 6 + SECTORS * q, 1, 2.0, 1)
    for r in range(1, 6):
        for q in range(sector):
            put(r, q, r + SECTORS * q, 0, 2.0, None)
            put(r, 128 + q, r + SECTORS * q, 1, 2.0, None)
    return split_bf16(forward) + split_bf16(inverse) + (waves.astype(np.int32),)


def combine(terms):
    groups = {}
    for coefficient, array in terms:
        size = round(abs(coefficient), 6)
        if size < 1e-6:
            continue
        groups.setdefault(size, []).append((coefficient, array))
    total = None
    for size in sorted(groups, reverse=True):
        part = None
        for coefficient, array in groups[size]:
            if part is None:
                part = array if coefficient > 0 else -array
            else:
                part = part + array if coefficient > 0 else part - array
        if size != 1.0:
            part = part * abs(groups[size][0][0])
        total = part if total is None else total + part
    return total


def cos12(i):
    return math.cos(2.0 * math.pi * (i % 12) / 12)


def sin12(i):
    return math.sin(2.0 * math.pi * (i % 12) / 12)


def sector_dft(x):
    sums = [None] + [x[j] + x[12 - j] for j in range(1, 6)]
    differences = [None] + [x[j] - x[12 - j] for j in range(1, 6)]
    real, imag = [], []
    for r in range(7):
        terms = [(1.0, x[0]), (1.0 if r % 2 == 0 else -1.0, x[6])]
        terms += [(cos12(j * r), sums[j]) for j in range(1, 6)]
        real.append(combine(terms))
        if 0 < r < 6:
            imag.append(combine([(-sin12(j * r), differences[j]) for j in range(1, 6)]))
        else:
            imag.append(None)
    return [(real[0], real[6])] + [(real[r], imag[r]) for r in range(1, 6)]


def sector_inverse(w):
    out = [None] * 12
    for j in range(7):
        terms = [(1.0, w[0][0]), (1.0 if j % 2 == 0 else -1.0, w[0][1])]
        terms += [(cos12(j * r), w[r][0]) for r in range(1, 6)]
        even = combine(terms)
        if j in (0, 6):
            out[j] = even
            continue
        odd = combine([(sin12(j * r), w[r][1]) for r in range(1, 6)])
        out[j] = even - odd
        out[12 - j] = even + odd
    return out


def split_dot(x, high, low):
    x_high = x.astype(jnp.bfloat16)
    x_low = (x - x_high.astype(jnp.float32)).astype(jnp.bfloat16)
    dot = functools.partial(jnp.dot, preferred_element_type=jnp.float32)
    return dot(x_high, high) + (dot(x_low, high) + dot(x_high, low))


def kernel(
    lat_count, fields, rows,
    q_hbm, u_hbm, v_hbm, cut_ref, fh_hbm, fl_hbm, ih_hbm, il_hbm, waves_ref,
    out_ref,
    q_in, u_in, v_in, q_pad, u_pad, v_pad, edge_out, edge_in, side_out, side_in,
    fh, fl, ih, il, stepped, land, done, result,
    load_sem, table_sem, halo_send, halo_recv, go_send, go_recv, back_send, back_recv,
):
    lat, lon = lax.axis_index("lat"), lax.axis_index("lon")
    chip, core = lon // 2, lax.rem(lon, 2)
    slabs = fields * rows
    tiles = 2 * slabs
    first = 15 * chip + 8 * core
    low_edge, high_edge = lat == 0, lat == lat_count - 1
    polar = jnp.logical_or(
        lat * rows < POLAR_ROWS, (lat_count - 1 - lat) * rows < POLAR_ROWS
    )
    across = lax.rem(lon + 6, SECTORS)
    north = (jnp.where(low_edge, 0, lat - 1), jnp.where(low_edge, across, lon))
    south = (jnp.where(high_edge, lat, lat + 1), jnp.where(high_edge, across, lon))
    west = (lat, lax.rem(lon + SECTORS - 1, SECTORS))
    east = (lat, lax.rem(lon + 1, SECTORS))

    loads = [
        pltpu.make_async_copy(q_hbm, q_in, load_sem.at[0]),
        pltpu.make_async_copy(u_hbm, u_in, load_sem.at[1]),
        pltpu.make_async_copy(v_hbm, v_in, load_sem.at[2]),
    ]
    for load in loads:
        load.start()
    tables = [
        pltpu.make_async_copy(source, target, table_sem.at[i])
        for i, (source, target) in enumerate(((fh_hbm, fh), (fl_hbm, fl), (ih_hbm, ih), (il_hbm, il)))
    ]

    barrier = pltpu.get_barrier_semaphore()
    for target in (north, south, west, east):
        pl.semaphore_signal(barrier, inc=1, device_id=target, device_id_type=MESH)

    @pl.when(polar)
    def _():
        for offset in range(2, SECTORS - 1):
            pl.semaphore_signal(
                barrier, inc=1, device_id=(lat, lax.rem(lon + offset, SECTORS)), device_id_type=MESH
            )
        for table in tables:
            table.start()

    for load in loads:
        load.wait()

    sector = q_in.shape[-1]
    lane = lax.broadcasted_iota(jnp.int32, (16, LANES), 1)
    east_pack = jnp.zeros((16, LANES), jnp.float32)
    west_pack = jnp.zeros((16, LANES), jnp.float32)
    for f in range(fields + 1):
        for r in range(rows):
            s = f * rows + r
            source, pad = (q_in.at[f], q_pad.at[f]) if f < fields else (u_in, u_pad)
            pad[r, :, pl.ds(0, sector)] = source[r]
            x = pad[r]
            west_pack = jnp.where(lane == s, pltpu.roll(x, s, 1), west_pack)
            east_pack = jnp.where(
                lane == s, pltpu.roll(x, (s - (sector - 1)) % LANES, 1), east_pack
            )
    for r in range(rows):
        v_pad[r, :, pl.ds(0, sector)] = v_in[r]
    side_out[0] = west_pack
    side_out[1] = east_pack
    for side, row in ((0, 0), (1, rows - 1)):
        for f in range(fields):
            edge_out[side, f] = q_pad[f, row]
        edge_out[side, fields] = v_pad[row]

    @pl.when(polar)
    def _():
        pl.semaphore_wait(barrier, 4 + SECTORS - 3)

    @pl.when(jnp.logical_not(polar))
    def _():
        pl.semaphore_wait(barrier, 4)

    def edge_copy(side, slot, target):
        return pltpu.make_async_remote_copy(
            src_ref=edge_out.at[side],
            dst_ref=edge_in.at[slot],
            send_sem=halo_send.at[side],
            recv_sem=halo_recv.at[slot],
            device_id=target,
            device_id_type=MESH,
        )

    to_north = edge_copy(0, jnp.where(low_edge, 0, 1), north)
    to_south = edge_copy(1, jnp.where(high_edge, 1, 0), south)
    to_west = pltpu.make_async_remote_copy(
        src_ref=side_out.at[0], dst_ref=side_in.at[1], send_sem=halo_send.at[2],
        recv_sem=halo_recv.at[2], device_id=west, device_id_type=MESH,
    )
    to_east = pltpu.make_async_remote_copy(
        src_ref=side_out.at[1], dst_ref=side_in.at[0], send_sem=halo_send.at[3],
        recv_sem=halo_recv.at[3], device_id=east, device_id_type=MESH,
    )
    for copy in (to_north, to_south, to_west, to_east):
        copy.start()
    to_west.wait_recv()
    to_east.wait_recv()
    edge_copy(0, 0, north).wait_recv()
    edge_copy(1, 1, south).wait_recv()

    from_west, from_east = side_in[0], side_in[1]

    def with_ghosts(x, s):
        x = jnp.where(lane == sector, pltpu.roll(from_east, (sector - s) % LANES, 1), x)
        return jnp.where(lane == LANES - 1, pltpu.roll(from_west, (LANES - 1 - s) % LANES, 1), x)

    flip_north = jnp.where(low_edge, -1.0, 1.0)
    flip_south = jnp.where(high_edge, -1.0, 1.0)
    for r in range(rows):
        u = with_ghosts(u_pad[r], fields * rows + r)
        east_speed = 0.5 * (u + pltpu.roll(u, LANES - 1, 1))
        west_speed = 0.5 * (pltpu.roll(u, 1, 1) + u)
        v = v_pad[r]
        v_next = v_pad[r + 1] if r < rows - 1 else edge_in[1, fields] * flip_south
        v_previous = v_pad[r - 1] if r > 0 else edge_in[0, fields] * flip_north
        south_speed = 0.5 * (v + v_next)
        north_speed = 0.5 * (v_previous + v)
        e_plus, e_minus = jnp.maximum(east_speed, 0.0), jnp.minimum(east_speed, 0.0)
        w_plus, w_minus = jnp.maximum(west_speed, 0.0), jnp.minimum(west_speed, 0.0)
        s_plus, s_minus = jnp.maximum(south_speed, 0.0), jnp.minimum(south_speed, 0.0)
        n_plus, n_minus = jnp.maximum(north_speed, 0.0), jnp.minimum(north_speed, 0.0)
        for f in range(fields):
            q = with_ghosts(q_pad[f, r], f * rows + r)
            q_next = q_pad[f, r + 1] if r < rows - 1 else edge_in[1, f]
            q_previous = q_pad[f, r - 1] if r > 0 else edge_in[0, f]
            east_flux = e_plus * q + e_minus * pltpu.roll(q, LANES - 1, 1)
            west_flux = w_plus * pltpu.roll(q, 1, 1) + w_minus * q
            south_flux = s_plus * q + s_minus * q_next
            north_flux = n_plus * q_previous + n_minus * q
            new = q - (east_flux - west_flux) - (south_flux - north_flux)
            new = jnp.where(lane < sector, new, 0.0)
            tile = 2 * (f * rows + r)
            stepped[tile] = new[:8]
            stepped[tile + 1] = new[8:]

    @pl.when(jnp.logical_not(polar))
    def _():
        out_ref[...] = stepped[pl.ds(0, tiles)]

    def peers():
        for offset in range(1, 6):
            for c in range(2):
                to_chip = lax.rem(chip + offset, 6)
                yield to_chip, c, 2 * to_chip + c

    def waiter(ref, sem):
        return pltpu.make_async_copy(ref, ref, sem)

    @pl.when(polar)
    def _():
        counts = ((4, 4), (4, 3))
        starts = (0, 4)

        def go(phase, to_first, count, to):
            pltpu.make_async_remote_copy(
                src_ref=stepped.at[pl.ds(to_first + starts[phase], count)],
                dst_ref=land.at[lon, pl.ds(starts[phase], count)],
                send_sem=go_send.at[phase], recv_sem=go_recv.at[phase],
                device_id=(lat, to), device_id_type=MESH,
            ).start()

        def back(phase, count, to):
            pltpu.make_async_remote_copy(
                src_ref=done.at[to, pl.ds(starts[phase], count)],
                dst_ref=result.at[pl.ds(first + starts[phase], count)],
                send_sem=back_send.at[phase], recv_sem=back_recv.at[phase],
                device_id=(lat, to), device_id_type=MESH,
            ).start()

        for phase in range(2):
            for to_chip, c, to in peers():
                go(phase, 15 * to_chip + 8 * c, counts[c][phase], to)
            for c in range(2):
                @pl.when(core == 1 - c)
                def _():
                    go(phase, 15 * chip + 8 * c, counts[c][phase], 2 * chip + c)

        land[lon] = stepped[pl.ds(first, 8)]
        for table in tables:
            table.wait()

        for phase in range(2):
            for c in range(2):
                @pl.when(core == c)
                def _():
                    count = counts[c][phase]
                    waiter(land.at[pl.ds(0, 11), pl.ds(0, count)], go_recv.at[phase]).wait()
            x = [land[j, pl.ds(starts[phase], 4)].reshape(32, LANES) for j in range(SECTORS)]
            limit = [cut_ref[lax.rem((first + starts[phase] + i) // 2, rows)] for i in range(4)]
            w = []
            for block, (a, b) in enumerate(sector_dft(x)):
                z = split_dot(jnp.concatenate([a, b], axis=1), fh[block], fl[block])
                wave = jnp.broadcast_to(waves_ref[pl.ds(block, 1)], (8, 256))
                z = jnp.concatenate(
                    [jnp.where(wave <= limit[i], z[8 * i : 8 * i + 8], 0.0) for i in range(4)], axis=0
                )
                y = split_dot(z, ih[block], il[block])
                w.append((y[:, :LANES], y[:, LANES:]))
            for j, y in enumerate(sector_inverse(w)):
                done[j, pl.ds(starts[phase], 4)] = y.reshape(4, 8, LANES)
            for c in range(2):
                @pl.when(core == c)
                def _():
                    count = counts[c][phase]
                    for _, _, to in peers():
                        back(phase, count, to)
                    back(phase, count, lon + 1 - 2 * c)
                    result[pl.ds(first + starts[phase], count)] = done[lon, pl.ds(starts[phase], count)]

        waiter(result.at[pl.ds(0, 44)], back_recv.at[0]).wait()
        for c in range(2):
            @pl.when(core == c)
            def _():
                waiter(result.at[pl.ds(0, 35 + counts[1 - c][1])], back_recv.at[1]).wait()
                waiter(stepped.at[pl.ds(0, 35 + counts[1 - c][1])], go_send.at[1]).wait()
                waiter(done.at[pl.ds(0, 11), pl.ds(0, counts[c][1])], back_send.at[1]).wait()
        waiter(stepped.at[pl.ds(0, 44)], go_send.at[0]).wait()
        waiter(done.at[pl.ds(0, 11), pl.ds(0, 4)], back_send.at[0]).wait()
        out_ref[...] = result[pl.ds(0, tiles)]

    for copy in (to_north, to_south, to_west, to_east):
        copy.wait_send()


def body(lat_count, tracers, zonal_wind, meridional_wind, cutoff):
    fields, levels, rows, sector = tracers.shape
    q = jnp.transpose(tracers, (0, 2, 1, 3))
    u = jnp.transpose(zonal_wind, (1, 0, 2))
    v = jnp.transpose(meridional_wind, (1, 0, 2))
    tables = [jnp.asarray(t) for t in dft_tables(SECTORS * sector, sector)]
    tiles = fields * rows * 2
    f32, bf16 = jnp.float32, jnp.bfloat16
    dma = pltpu.SemaphoreType.DMA
    anywhere = pl.BlockSpec(memory_space=pl.ANY)
    vmem = pl.BlockSpec(memory_space=pltpu.VMEM)
    out = pl.pallas_call(
        functools.partial(kernel, lat_count, fields, rows),
        out_shape=jax.ShapeDtypeStruct((tiles, 8, LANES), f32),
        in_specs=[anywhere] * 3 + [pl.BlockSpec(memory_space=pltpu.SMEM)] + [anywhere] * 4 + [vmem],
        out_specs=vmem,
        scratch_shapes=[
            pltpu.VMEM((fields, rows, levels, sector), f32),
            pltpu.VMEM((rows, levels, sector), f32),
            pltpu.VMEM((rows, levels, sector), f32),
            pltpu.VMEM((fields, rows, levels, LANES), f32),
            pltpu.VMEM((rows, levels, LANES), f32),
            pltpu.VMEM((rows, levels, LANES), f32),
            pltpu.VMEM((2, fields + 1, levels, LANES), f32),
            pltpu.VMEM((2, fields + 1, levels, LANES), f32),
            pltpu.VMEM((2, levels, LANES), f32),
            pltpu.VMEM((2, levels, LANES), f32),
            pltpu.VMEM((6, 256, 256), bf16),
            pltpu.VMEM((6, 256, 256), bf16),
            pltpu.VMEM((6, 256, 256), bf16),
            pltpu.VMEM((6, 256, 256), bf16),
            pltpu.VMEM((96, 8, LANES), f32),
            pltpu.VMEM((SECTORS, 8, 8, LANES), f32),
            pltpu.VMEM((SECTORS, 8, 8, LANES), f32),
            pltpu.VMEM((96, 8, LANES), f32),
            dma((3,)), dma((4,)), dma((4,)), dma((4,)), dma((2,)), dma((2,)), dma((2,)), dma((2,)),
        ],
        compiler_params=pltpu.CompilerParams(
            collective_id=0, has_side_effects=True, vmem_limit_bytes=40 * 1024 * 1024
        ),
    )(q, u, v, cutoff, *tables)
    out = out.reshape(fields, rows, levels, LANES)[..., :sector]
    return jnp.transpose(out, (0, 2, 1, 3))


def solution(mesh):
    in_specs = (P(None, None, "lat", "lon"), P(None, "lat", "lon"), P(None, "lat", "lon"), P("lat"))
    out_specs = P(None, None, "lat", "lon")
    return jax.shard_map(
        functools.partial(body, mesh.shape["lat"]),
        mesh=mesh, in_specs=in_specs, out_specs=out_specs, check_vma=False,
    )
```

time: 134 us -> 59.9 us (0.45)
  the two profiles are of different devices: /device:TPU:57 before, /device:TPU:63 now
where the time goes in v1:
time: 59.9 us; the launch traced here: 59.4 us
  Pallas kernels  50.6 us (84%)
  local copies, waits for them, and re-layouts  8.75 us (15%)
    pallas_call x1, Pallas kernels, body(): pl.pallas_call(functools.partial(kernel, lat_count, fields, rows), out_sh...  50.6 us
    unnamed x18, local copies, waits for them, and re-layouts  7.98 us

profile of v1, /device:TPU:63, one launch (start us, length us, event | category | flops | bytes accessed | tf_op | source)
XLA Modules:
  0.0 59.4 jit_solution(6982117846999675043)
XLA Ops:
  0.0 0.0 copy-start.7
  0.0 0.0 copy-start.8
  0.0 0.7 %copy-done.7 = s32[8,256]{1,0:T(8,128)S(1)} copy-done((s32[8,256]{1,0:T(8,128)S(1)}, s32[8,256]{1,0:T(8,128)}, u32[]{:S(2)}) %copy-start.7) | copy-done | bytes 8216
  0.7 0.0 copy-done.8
  0.7 0.0 copy-start
  0.7 1.1 %copy-done = bf16[6,256,256]{2,1,0:T(8,128)(2,1)S(1)} copy-done((bf16[6,256,256]{2,1,0:T(8,128)(2,1)S(1)}, bf16[6,256,256]{2,1,0:T(8,128)(2,1)}, u32[]{:S(2)}) %copy-start) | copy-done | bytes 786456
  1.8 0.0 copy-start.1
  1.8 1.1 %copy-done.1 = bf16[6,256,256]{2,1,0:T(8,128)(2,1)S(1)} copy-done((bf16[6,256,256]{2,1,0:T(8,128)(2,1)S(1)}, bf16[6,256,256]{2,1,0:T(8,128)(2,1)}, u32[]{:S(2)}) %copy-start.1) | copy-done | bytes 786456
  3.0 0.0 copy-start.2
  3.0 1.1 %copy-done.2 = bf16[6,256,256]{2,1,0:T(8,128)(2,1)S(1)} copy-done((bf16[6,256,256]{2,1,0:T(8,128)(2,1)S(1)}, bf16[6,256,256]{2,1,0:T(8,128)(2,1)}, u32[]{:S(2)}) %copy-start.2) | copy-done | bytes 786456
  4.1 0.0 copy-start.3
  4.1 1.1 %copy-done.3 = bf16[6,256,256]{2,1,0:T(8,128)(2,1)S(1)} copy-done((bf16[6,256,256]{2,1,0:T(8,128)(2,1)S(1)}, bf16[6,256,256]{2,1,0:T(8,128)(2,1)}, u32[]{:S(2)}) %copy-start.3) | copy-done | bytes 786456
  5.2 0.0 copy-start.4
  5.2 1.0 %copy-done.4 = f32[5,16,9,120]{3,1,2,0:T(8,128)S(1)} copy-done((f32[5,16,9,120]{3,1,2,0:T(8,128)S(1)}, f32[5,16,9,120]{3,1,2,0:T(8,128)}, u32[]{:S(2)}) %copy-start.4) | copy-done | bytes 345624
  6.2 0.0 copy-start.5
  6.2 0.9 %copy-done.5 = f32[16,9,120]{2,0,1:T(8,128)S(1)} copy-done((f32[16,9,120]{2,0,1:T(8,128)S(1)}, f32[16,9,120]{2,0,1:T(8,128)}, u32[]{:S(2)}) %copy-start.5) | copy-done | bytes 69144
  7.1 0.0 copy-start.6
  7.1 0.9 %copy-done.6 = f32[16,9,120]{2,0,1:T(8,128)S(1)} copy-done((f32[16,9,120]{2,0,1:T(8,128)S(1)}, f32[16,9,120]{2,0,1:T(8,128)}, u32[]{:S(2)}) %copy-start.6) | copy-done | bytes 69144
  8.0 50.6 %shard_map.91 = f32[90,8,128]{2,1,0:T(8,128)S(1)} custom-call(f32[5,9,16,120]{3,2,1,0:T(8,128)S(1)} %bitcast.7, f32[9,16,120]{2,1,0:T(8,128)S(1)} %bitcast.8, f32[9,16,120]{2,1,0:T(8,128)S(1)} %bitcast.9, s32[9]{0:T(128)S(1)} %copy-done.8, bf16[6,256,256]{2,1,0:T(8,128)(2,1)S(1)} %copy-done.3, bf16[6,256,256]{2,1,0:T(8,128)(2,1)S(1)} %copy-done.2, ...), custom_call_target="tpu_custom_call" | custom-call | tf_op jit(solution)/shard_map/pallas_call | solution.py:378
  58.6 0.8 %slice_bitcast_fusion = f32[5,16,9,120]{3,1,2,0:T(8,128)} fusion(f32[5,9,16,128]{3,2,1,0:T(8,128)S(1)} %bitcast.6), kind=kLoop, calls=%fused_computation | loop fusion | bytes 691200 | tf_op jit(solution)/shard_map/transpose | solution.py:409
Async XLA Ops:
  0.0 0.7 %copy-start.7 = (s32[8,256]{1,0:T(8,128)S(1)}, s32[8,256]{1,0:T(8,128)}, u32[]{:S(2)}) copy-start(s32[8,256]{1,0:T(8,128)} %constant.14.clone.waves_ref) | copy-start | bytes 24580
  0.0 0.7 %copy-start.8 = (s32[9]{0:T(128)S(1)}, s32[9]{0:T(128)}, u32[]{:S(2)}) copy-start(s32[9]{0:T(128)} %cut_ref.1) | copy-start | bytes 112
  0.7 1.1 %copy-start = (bf16[6,256,256]{2,1,0:T(8,128)(2,1)S(1)}, bf16[6,256,256]{2,1,0:T(8,128)(2,1)}, u32[]{:S(2)}) copy-start(bf16[6,256,256]{2,1,0:T(8,128)(2,1)} %constant.13.clone.il_hbm) | copy-start | bytes 2359300
  1.8 1.1 %copy-start.1 = (bf16[6,256,256]{2,1,0:T(8,128)(2,1)S(1)}, bf16[6,256,256]{2,1,0:T(8,128)(2,1)}, u32[]{:S(2)}) copy-start(bf16[6,256,256]{2,1,0:T(8,128)(2,1)} %constant.12.clone.ih_hbm) | copy-start | bytes 2359300
  3.0 1.1 %copy-start.2 = (bf16[6,256,256]{2,1,0:T(8,128)(2,1)S(1)}, bf16[6,256,256]{2,1,0:T(8,128)(2,1)}, u32[]{:S(2)}) copy-start(bf16[6,256,256]{2,1,0:T(8,128)(2,1)} %constant.11.clone.fl_hbm) | copy-start | bytes 2359300
  4.1 1.1 %copy-start.3 = (bf16[6,256,256]{2,1,0:T(8,128)(2,1)S(1)}, bf16[6,256,256]{2,1,0:T(8,128)(2,1)}, u32[]{:S(2)}) copy-start(bf16[6,256,256]{2,1,0:T(8,128)(2,1)} %constant.10.clone.fh_hbm) | copy-start | bytes 2359300
  5.2 1.0 %copy-start.4 = (f32[5,16,9,120]{3,1,2,0:T(8,128)S(1)}, f32[5,16,9,120]{3,1,2,0:T(8,128)}, u32[]{:S(2)}) copy-start(f32[5,16,9,120]{3,1,2,0:T(8,128)} %param.9) | copy-start | bytes 1036804
  6.2 0.9 %copy-start.5 = (f32[16,9,120]{2,0,1:T(8,128)S(1)}, f32[16,9,120]{2,0,1:T(8,128)}, u32[]{:S(2)}) copy-start(f32[16,9,120]{2,0,1:T(8,128)} %param.10) | copy-start | bytes 207364
  7.1 0.9 %copy-start.6 = (f32[16,9,120]{2,0,1:T(8,128)S(1)}, f32[16,9,120]{2,0,1:T(8,128)}, u32[]{:S(2)}) copy-start(f32[16,9,120]{2,0,1:T(8,128)} %param.11) | copy-start | bytes 207364

commit v2 on v1

--- a/solution.py
+++ b/solution.py
@@ -133,10 +133,10 @@
 
 def kernel(
     lat_count, fields, rows,
-    q_hbm, u_hbm, v_hbm, cut_ref, fh_hbm, fl_hbm, ih_hbm, il_hbm, waves_ref,
+    q_hbm, u_hbm, v_hbm, cut_hbm, fh_hbm, fl_hbm, ih_hbm, il_hbm, waves_hbm,
     out_ref,
     q_in, u_in, v_in, q_pad, u_pad, v_pad, edge_out, edge_in, side_out, side_in,
-    fh, fl, ih, il, stepped, land, done, result,
+    fh, fl, ih, il, waves_ref, cut_ref, stepped, land, done, result,
     load_sem, table_sem, halo_send, halo_recv, go_send, go_recv, back_send, back_recv,
 ):
     lat, lon = lax.axis_index("lat"), lax.axis_index("lon")
@@ -163,7 +163,9 @@
         load.start()
     tables = [
         pltpu.make_async_copy(source, target, table_sem.at[i])
-        for i, (source, target) in enumerate(((fh_hbm, fh), (fl_hbm, fl), (ih_hbm, ih), (il_hbm, il)))
+        for i, (source, target) in enumerate(
+            ((fh_hbm, fh), (fl_hbm, fl), (ih_hbm, ih), (il_hbm, il), (waves_hbm, waves_ref), (cut_hbm, cut_ref))
+        )
     ]
 
     barrier = pltpu.get_barrier_semaphore()
@@ -373,12 +375,12 @@
     tiles = fields * rows * 2
     f32, bf16 = jnp.float32, jnp.bfloat16
     dma = pltpu.SemaphoreType.DMA
-    anywhere = pl.BlockSpec(memory_space=pl.ANY)
+    hbm = pl.BlockSpec(memory_space=pltpu.HBM)
     vmem = pl.BlockSpec(memory_space=pltpu.VMEM)
     out = pl.pallas_call(
         functools.partial(kernel, lat_count, fields, rows),
         out_shape=jax.ShapeDtypeStruct((tiles, 8, LANES), f32),
-        in_specs=[anywhere] * 3 + [pl.BlockSpec(memory_space=pltpu.SMEM)] + [anywhere] * 4 + [vmem],
+        in_specs=[hbm] * 9,
         out_specs=vmem,
         scratch_shapes=[
             pltpu.VMEM((fields, rows, levels, sector), f32),
@@ -395,14 +397,16 @@
             pltpu.VMEM((6, 256, 256), bf16),
             pltpu.VMEM((6, 256, 256), bf16),
             pltpu.VMEM((6, 256, 256), bf16),
+            pltpu.VMEM((8, 256), jnp.int32),
+            pltpu.SMEM((rows,), jnp.int32),
             pltpu.VMEM((96, 8, LANES), f32),
             pltpu.VMEM((SECTORS, 8, 8, LANES), f32),
             pltpu.VMEM((SECTORS, 8, 8, LANES), f32),
             pltpu.VMEM((96, 8, LANES), f32),
-            dma((3,)), dma((4,)), dma((4,)), dma((4,)), dma((2,)), dma((2,)), dma((2,)), dma((2,)),
+            dma((3,)), dma((6,)), dma((4,)), dma((4,)), dma((2,)), dma((2,)), dma((2,)), dma((2,)),
         ],
         compiler_params=pltpu.CompilerParams(
-            collective_id=0, has_side_effects=True, vmem_limit_bytes=40 * 1024 * 1024
+            collective_id=0, has_side_effects=True, vmem_limit_bytes=60 * 1024 * 1024
         ),
     )(q, u, v, cutoff, *tables)
     out = out.reshape(fields, rows, levels, LANES)[..., :sector]

time: 59.9 us -> 52.4 us (0.87)
  local copies, waits for them, and re-layouts: 8.75 us -> 1.75 us
    unnamed x18 -> x0, local copies, waits for them, and re-layouts: 7.98 us -> none
    transpose x1, local copies, waits for them, and re-layouts: 0.76 us -> 1.75 us  [body(): return jnp.transpose(out, (0, 2, 1, 3))]
where the time goes in v2:
time: 52.4 us; the launch traced here: 52.2 us
  Pallas kernels  50.5 us (96%)
  local copies, waits for them, and re-layouts  1.75 us (3%)
    pallas_call x1, Pallas kernels, body(): pl.pallas_call(functools.partial(kernel, lat_count, fields, rows), out_sh...  50.5 us
    transpose x1, local copies, waits for them, and re-layouts, body(): return jnp.transpose(out, (0, 2, 1, 3))  1.75 us

profile of v2, /device:TPU:63, one launch (start us, length us, event | category | flops | bytes accessed | tf_op | source)
XLA Modules:
  0.0 52.2 jit_solution(295428763464192374)
XLA Ops:
  0.0 50.5 %shard_map.91 = f32[90,8,128]{2,1,0:T(8,128)} custom-call(f32[5,9,16,120]{3,2,1,0:T(8,128)} %bitcast.7, f32[9,16,120]{2,1,0:T(8,128)} %bitcast.8, f32[9,16,120]{2,1,0:T(8,128)} %bitcast.9, s32[9]{0:T(128)} %cut_hbm.1, bf16[6,256,256]{2,1,0:T(8,128)(2,1)} %constant.10.clone.fh_hbm, bf16[6,256,256]{2,1,0:T(8,128)(2,1)} %constant.11.clone.fl_hbm, ...), custom_call_target="tpu_custom_call" | custom-call | tf_op jit(solution)/shard_map/pallas_call | solution.py:380
  50.5 1.7 %slice_bitcast_fusion = f32[5,16,9,120]{3,1,2,0:T(8,128)} fusion(f32[5,9,16,128]{3,2,1,0:T(8,128)} %bitcast.6), kind=kLoop, calls=%fused_computation | loop fusion | bytes 691200 | tf_op jit(solution)/shard_map/transpose | solution.py:413

commit v3 on v2

--- a/solution.py
+++ b/solution.py
@@ -14,6 +14,7 @@
 POLAR_ROWS = 96
 SECTORS = 12
 LANES = 128
+STRIDE = 16
 
 
 def split_bf16(table):
@@ -62,7 +63,7 @@
         for q in range(sector):
             put(r, q, r + SECTORS * q, 0, 2.0, None)
             put(r, 128 + q, r + SECTORS * q, 1, 2.0, None)
-    return split_bf16(forward) + split_bf16(inverse) + (waves.astype(np.int32),)
+    return split_bf16(forward) + split_bf16(inverse) + (waves.astype(np.float32),)
 
 
 def combine(terms):
@@ -136,23 +137,49 @@
     q_hbm, u_hbm, v_hbm, cut_hbm, fh_hbm, fl_hbm, ih_hbm, il_hbm, waves_hbm,
     out_ref,
     q_in, u_in, v_in, q_pad, u_pad, v_pad, edge_out, edge_in, side_out, side_in,
-    fh, fl, ih, il, waves_ref, cut_ref, stepped, land, done, result,
-    load_sem, table_sem, halo_send, halo_recv, go_send, go_recv, back_send, back_recv,
+    fh, fl, ih, il, waves_ref, cut_ref, cut_out, cut_rows, stepped, relay, land, done, result,
+    load_sem, table_sem, halo_send, halo_recv, cut_send, cut_recv, relay_send, relay_recv,
+    go_send, go_recv, back_send, back_recv,
 ):
     lat, lon = lax.axis_index("lat"), lax.axis_index("lon")
     chip, core = lon // 2, lax.rem(lon, 2)
-    slabs = fields * rows
-    tiles = 2 * slabs
-    first = 15 * chip + 8 * core
+    tiles = 2 * fields * rows
     low_edge, high_edge = lat == 0, lat == lat_count - 1
-    polar = jnp.logical_or(
-        lat * rows < POLAR_ROWS, (lat_count - 1 - lat) * rows < POLAR_ROWS
+    caps = -(-POLAR_ROWS // rows)
+    in_north, in_south = lat < caps, lat >= lat_count - caps
+    main = jnp.logical_or(in_north, in_south)
+    helper = jnp.logical_or(
+        jnp.logical_and(lat >= STRIDE, lat < STRIDE + caps),
+        jnp.logical_and(lat >= lat_count - STRIDE - caps, lat < lat_count - STRIDE),
     )
+    mate = jnp.where(jnp.logical_or(in_north, lat >= lat_count // 2), STRIDE, -STRIDE)
+    mate = lat + jnp.where(in_south, -STRIDE, mate)
+    team = jnp.where(main, lat, mate)
     across = lax.rem(lon + 6, SECTORS)
     north = (jnp.where(low_edge, 0, lat - 1), jnp.where(low_edge, across, lon))
     south = (jnp.where(high_edge, lat, lat + 1), jnp.where(high_edge, across, lon))
     west = (lat, lax.rem(lon + SECTORS - 1, SECTORS))
     east = (lat, lax.rem(lon + 1, SECTORS))
+    slot = jnp.where(chip < 3, 2 * chip, 11 - 2 * chip)
+    starts = (
+        jnp.where(main, 2 * lon, 48 + 4 * slot + 2 * core),
+        jnp.where(main, 24 + 2 * lon, 72 + 3 * slot + 2 * core),
+    )
+
+    def turned(offset):
+        return lax.rem(lon + offset, SECTORS)
+
+    def greet(target):
+        pl.semaphore_signal(barrier, inc=1, device_id=target, device_id_type=MESH)
+
+    def waiter(ref, sem):
+        return pltpu.make_async_copy(ref, ref, sem)
+
+    def send(source, target, send_sem, recv_sem, device):
+        pltpu.make_async_remote_copy(
+            src_ref=source, dst_ref=target, send_sem=send_sem, recv_sem=recv_sem,
+            device_id=device, device_id_type=MESH,
+        ).start()
 
     loads = [
         pltpu.make_async_copy(q_hbm, q_in, load_sem.at[0]),
@@ -164,22 +191,29 @@
     tables = [
         pltpu.make_async_copy(source, target, table_sem.at[i])
         for i, (source, target) in enumerate(
-            ((fh_hbm, fh), (fl_hbm, fl), (ih_hbm, ih), (il_hbm, il), (waves_hbm, waves_ref), (cut_hbm, cut_ref))
+            ((cut_hbm, cut_ref), (waves_hbm, waves_ref), (fh_hbm, fh), (fl_hbm, fl), (ih_hbm, ih), (il_hbm, il))
         )
     ]
 
     barrier = pltpu.get_barrier_semaphore()
     for target in (north, south, west, east):
-        pl.semaphore_signal(barrier, inc=1, device_id=target, device_id_type=MESH)
-
-    @pl.when(polar)
+        greet(target)
+
+    @pl.when(jnp.logical_or(main, helper))
     def _():
         for offset in range(2, SECTORS - 1):
-            pl.semaphore_signal(
-                barrier, inc=1, device_id=(lat, lax.rem(lon + offset, SECTORS)), device_id_type=MESH
-            )
+            greet((lat, turned(offset)))
         for table in tables:
             table.start()
+
+    @pl.when(main)
+    def _():
+        for offset in range(SECTORS):
+            greet((mate, turned(offset)))
+
+    @pl.when(helper)
+    def _():
+        greet((mate, lon))
 
     for load in loads:
         load.wait()
@@ -207,11 +241,15 @@
             edge_out[side, f] = q_pad[f, row]
         edge_out[side, fields] = v_pad[row]
 
-    @pl.when(polar)
-    def _():
-        pl.semaphore_wait(barrier, 4 + SECTORS - 3)
-
-    @pl.when(jnp.logical_not(polar))
+    @pl.when(main)
+    def _():
+        pl.semaphore_wait(barrier, 4 + SECTORS - 3 + 1)
+
+    @pl.when(helper)
+    def _():
+        pl.semaphore_wait(barrier, 4 + SECTORS - 3 + SECTORS)
+
+    @pl.when(jnp.logical_not(jnp.logical_or(main, helper)))
     def _():
         pl.semaphore_wait(barrier, 4)
 
@@ -237,6 +275,41 @@
     )
     for copy in (to_north, to_south, to_west, to_east):
         copy.start()
+
+    @pl.when(main)
+    def _():
+        tables[0].wait()
+        for r in range(rows):
+            limit = jnp.full((1, LANES), cut_ref[r], jnp.int32).astype(jnp.float32)
+            cut_out[pl.ds(r, 1)] = limit
+            cut_rows[pl.ds(r, 1)] = limit
+        cut_out[pl.ds(rows, 16 - rows)] = jnp.zeros((16 - rows, LANES), jnp.float32)
+        send(cut_out, cut_rows, cut_send, cut_recv, (mate, lon))
+
+    @pl.when(helper)
+    def _():
+        for phase in range(2):
+            for group in range(3):
+                count = (8, 6)[phase]
+                chunk = relay.at[pl.ds(24 * phase + count * group, count)]
+                waiter(chunk, relay_recv.at[3 * phase + group]).wait()
+                for place, to_chip in enumerate((group, 5 - group)):
+                    for c in range(2):
+                        to = 2 * to_chip + c
+                        n = 2 - phase * c
+                        at = 24 * phase + count * group + count // 2 * place + 2 * c
+
+                        @pl.when(lon != to)
+                        def _():
+                            send(
+                                relay.at[pl.ds(at, n)], land.at[lon, pl.ds(2 * phase, n)],
+                                go_send.at[phase], go_recv.at[phase], (lat, to),
+                            )
+
+                        @pl.when(lon == to)
+                        def _():
+                            land[lon, pl.ds(2 * phase, n)] = relay[pl.ds(at, n)]
+
     to_west.wait_recv()
     to_east.wait_recv()
     edge_copy(0, 0, north).wait_recv()
@@ -277,90 +350,99 @@
             stepped[tile] = new[:8]
             stepped[tile + 1] = new[8:]
 
-    @pl.when(jnp.logical_not(polar))
-    def _():
-        out_ref[...] = stepped[pl.ds(0, tiles)]
-
-    def peers():
-        for offset in range(1, 6):
-            for c in range(2):
-                to_chip = lax.rem(chip + offset, 6)
-                yield to_chip, c, 2 * to_chip + c
-
-    def waiter(ref, sem):
-        return pltpu.make_async_copy(ref, ref, sem)
-
-    @pl.when(polar)
-    def _():
-        counts = ((4, 4), (4, 3))
-        starts = (0, 4)
-
-        def go(phase, to_first, count, to):
-            pltpu.make_async_remote_copy(
-                src_ref=stepped.at[pl.ds(to_first + starts[phase], count)],
-                dst_ref=land.at[lon, pl.ds(starts[phase], count)],
-                send_sem=go_send.at[phase], recv_sem=go_recv.at[phase],
-                device_id=(lat, to), device_id_type=MESH,
-            ).start()
-
-        def back(phase, count, to):
-            pltpu.make_async_remote_copy(
-                src_ref=done.at[to, pl.ds(starts[phase], count)],
-                dst_ref=result.at[pl.ds(first + starts[phase], count)],
-                send_sem=back_send.at[phase], recv_sem=back_recv.at[phase],
-                device_id=(lat, to), device_id_type=MESH,
-            ).start()
-
+    @pl.when(jnp.logical_not(main))
+    def _():
+        out_ref[...] = stepped[...]
+
+    @pl.when(main)
+    def _():
         for phase in range(2):
-            for to_chip, c, to in peers():
-                go(phase, 15 * to_chip + 8 * c, counts[c][phase], to)
-            for c in range(2):
-                @pl.when(core == 1 - c)
+            for group in range(3):
+                count = (8, 6)[phase]
+                at = 24 * phase + count * group
+                send(
+                    stepped.at[pl.ds(48 + at, count)], relay.at[pl.ds(at, count)],
+                    relay_send, relay_recv.at[3 * phase + group], (mate, lon),
+                )
+            for offset in range(1, SECTORS):
+                to = turned(offset)
+                send(
+                    stepped.at[pl.ds(24 * phase + 2 * to, 2)], land.at[lon, pl.ds(2 * phase, 2)],
+                    go_send.at[phase], go_recv.at[phase], (lat, to),
+                )
+            land[lon, pl.ds(2 * phase, 2)] = stepped[pl.ds(24 * phase + 2 * lon, 2)]
+
+    @pl.when(helper)
+    def _():
+        waiter(cut_rows, cut_recv).wait()
+        tables[0].wait()
+
+    @pl.when(jnp.logical_or(main, helper))
+    def _():
+        short = jnp.logical_and(helper, core == 1)
+        for table in tables[1:]:
+            table.wait()
+        for phase in range(2):
+            for n in range(1, 3) if phase else (2,):
+                @pl.when(short == (n == 1) if phase else core >= 0)
                 def _():
-                    go(phase, 15 * chip + 8 * c, counts[c][phase], 2 * chip + c)
-
-        land[lon] = stepped[pl.ds(first, 8)]
-        for table in tables:
-            table.wait()
-
-        for phase in range(2):
-            for c in range(2):
-                @pl.when(core == c)
-                def _():
-                    count = counts[c][phase]
-                    waiter(land.at[pl.ds(0, 11), pl.ds(0, count)], go_recv.at[phase]).wait()
-            x = [land[j, pl.ds(starts[phase], 4)].reshape(32, LANES) for j in range(SECTORS)]
-            limit = [cut_ref[lax.rem((first + starts[phase] + i) // 2, rows)] for i in range(4)]
+                    waiter(land.at[pl.ds(0, 11), pl.ds(0, n)], go_recv.at[phase]).wait()
+            x = [land[j, pl.ds(2 * phase, 2)].reshape(16, LANES) for j in range(SECTORS)]
+            limits = []
+            for i in range(2):
+                row = lax.rem((starts[phase] + i) // 2, rows)
+                limit = jnp.broadcast_to(cut_rows[pl.ds(row, 1)], (8, LANES))
+                limits.append(jnp.concatenate([limit, limit], axis=1))
+            limits = jnp.concatenate(limits, axis=0)
             w = []
             for block, (a, b) in enumerate(sector_dft(x)):
                 z = split_dot(jnp.concatenate([a, b], axis=1), fh[block], fl[block])
-                wave = jnp.broadcast_to(waves_ref[pl.ds(block, 1)], (8, 256))
-                z = jnp.concatenate(
-                    [jnp.where(wave <= limit[i], z[8 * i : 8 * i + 8], 0.0) for i in range(4)], axis=0
-                )
+                wave = jnp.broadcast_to(waves_ref[pl.ds(block, 1)], (16, 256))
+                z = jnp.where(wave <= limits, z, 0.0)
                 y = split_dot(z, ih[block], il[block])
                 w.append((y[:, :LANES], y[:, LANES:]))
             for j, y in enumerate(sector_inverse(w)):
-                done[j, pl.ds(starts[phase], 4)] = y.reshape(4, 8, LANES)
-            for c in range(2):
-                @pl.when(core == c)
+                done[j, pl.ds(2 * phase, 2)] = y.reshape(2, 8, LANES)
+            for n in range(1, 3) if phase else (2,):
+                @pl.when(short == (n == 1) if phase else core >= 0)
                 def _():
-                    count = counts[c][phase]
-                    for _, _, to in peers():
-                        back(phase, count, to)
-                    back(phase, count, lon + 1 - 2 * c)
-                    result[pl.ds(first + starts[phase], count)] = done[lon, pl.ds(starts[phase], count)]
-
-        waiter(result.at[pl.ds(0, 44)], back_recv.at[0]).wait()
+                    def back(to):
+                        send(
+                            done.at[to, pl.ds(2 * phase, n)], result.at[pl.ds(starts[phase], n)],
+                            back_send.at[phase], back_recv.at[phase], (team, to),
+                        )
+
+                    for offset in range(1, SECTORS):
+                        back(turned(offset))
+
+                    @pl.when(helper)
+                    def _():
+                        back(lon)
+
+            @pl.when(main)
+            def _():
+                result[pl.ds(starts[phase], 2)] = done[lon, pl.ds(2 * phase, 2)]
+
+    @pl.when(main)
+    def _():
+        waiter(result.at[pl.ds(0, 46)], back_recv.at[0]).wait()
+        waiter(result.at[pl.ds(0, 40)], back_recv.at[1]).wait()
+        out_ref[...] = result[...]
+        for phase in range(2):
+            waiter(stepped.at[pl.ds(0, 22)], go_send.at[phase]).wait()
+            waiter(stepped.at[pl.ds(0, 22)], back_send.at[phase]).wait()
+        waiter(stepped.at[pl.ds(0, 42)], relay_send).wait()
+        waiter(cut_out, cut_send).wait()
+
+    @pl.when(helper)
+    def _():
+        waiter(stepped.at[pl.ds(0, 22)], go_send.at[0]).wait()
+        waiter(stepped.at[pl.ds(0, 24)], back_send.at[0]).wait()
         for c in range(2):
             @pl.when(core == c)
             def _():
-                waiter(result.at[pl.ds(0, 35 + counts[1 - c][1])], back_recv.at[1]).wait()
-                waiter(stepped.at[pl.ds(0, 35 + counts[1 - c][1])], go_send.at[1]).wait()
-                waiter(done.at[pl.ds(0, 11), pl.ds(0, counts[c][1])], back_send.at[1]).wait()
-        waiter(stepped.at[pl.ds(0, 44)], go_send.at[0]).wait()
-        waiter(done.at[pl.ds(0, 11), pl.ds(0, 4)], back_send.at[0]).wait()
-        out_ref[...] = result[pl.ds(0, tiles)]
+                waiter(stepped.at[pl.ds(0, 16 + c)], go_send.at[1]).wait()
+                waiter(stepped.at[pl.ds(0, 24 - 12 * c)], back_send.at[1]).wait()
 
     for copy in (to_north, to_south, to_west, to_east):
         copy.wait_send()
@@ -397,13 +479,17 @@
             pltpu.VMEM((6, 256, 256), bf16),
             pltpu.VMEM((6, 256, 256), bf16),
             pltpu.VMEM((6, 256, 256), bf16),
-            pltpu.VMEM((8, 256), jnp.int32),
+            pltpu.VMEM((8, 256), f32),
             pltpu.SMEM((rows,), jnp.int32),
-            pltpu.VMEM((96, 8, LANES), f32),
-            pltpu.VMEM((SECTORS, 8, 8, LANES), f32),
-            pltpu.VMEM((SECTORS, 8, 8, LANES), f32),
-            pltpu.VMEM((96, 8, LANES), f32),
-            dma((3,)), dma((6,)), dma((4,)), dma((4,)), dma((2,)), dma((2,)), dma((2,)), dma((2,)),
+            pltpu.VMEM((16, LANES), f32),
+            pltpu.VMEM((16, LANES), f32),
+            pltpu.VMEM((tiles, 8, LANES), f32),
+            pltpu.VMEM((42, 8, LANES), f32),
+            pltpu.VMEM((SECTORS, 4, 8, LANES), f32),
+            pltpu.VMEM((SECTORS, 4, 8, LANES), f32),
+            pltpu.VMEM((tiles, 8, LANES), f32),
+            dma((3,)), dma((6,)), dma((4,)), dma((4,)), dma, dma, dma, dma((6,)),
+            dma((2,)), dma((2,)), dma((2,)), dma((2,)),
         ],
         compiler_params=pltpu.CompilerParams(
             collective_id=0, has_side_effects=True, vmem_limit_bytes=60 * 1024 * 1024

time: 52.4 us -> 45.4 us (0.87)
  Pallas kernels: 50.5 us -> 43.5 us
    pallas_call x1, Pallas kernels: 50.5 us -> 43.5 us  [body(): pl.pallas_call(functools.partial(kernel, lat_count, fields, rows), out_sh...]
where the time goes in v3:
time: 45.4 us; the launch traced here: 45.3 us
  Pallas kernels  43.5 us (96%)
  local copies, waits for them, and re-layouts  1.75 us (4%)
    pallas_call x1, Pallas kernels, body(): pl.pallas_call(functools.partial(kernel, lat_count, fields, rows), out_sh...  43.5 us
    transpose x1, local copies, waits for them, and re-layouts, body(): return jnp.transpose(out, (0, 2, 1, 3))  1.75 us

profile of v3, /device:TPU:63, one launch (start us, length us, event | category | flops | bytes accessed | tf_op | source)
XLA Modules:
  0.0 45.3 jit_solution(9300140511516064620)
XLA Ops:
  0.0 43.5 %shard_map.91 = f32[90,8,128]{2,1,0:T(8,128)} custom-call(f32[5,9,16,120]{3,2,1,0:T(8,128)} %bitcast.7, f32[9,16,120]{2,1,0:T(8,128)} %bitcast.8, f32[9,16,120]{2,1,0:T(8,128)} %bitcast.9, s32[9]{0:T(128)} %cut_hbm.1, bf16[6,256,256]{2,1,0:T(8,128)(2,1)} %constant.10.clone.fh_hbm, bf16[6,256,256]{2,1,0:T(8,128)(2,1)} %constant.11.clone.fl_hbm, ...), custom_call_target="tpu_custom_call" | custom-call | tf_op jit(solution)/shard_map/pallas_call | solution.py:462
  43.5 1.7 %slice_bitcast_fusion = f32[5,16,9,120]{3,1,2,0:T(8,128)} fusion(f32[5,9,16,128]{3,2,1,0:T(8,128)} %bitcast.6), kind=kLoop, calls=%fused_computation | loop fusion | bytes 691200 | tf_op jit(solution)/shard_map/transpose | solution.py:499

commit v4 on v3

--- a/solution.py
+++ b/solution.py
@@ -15,6 +15,12 @@
 SECTORS = 12
 LANES = 128
 STRIDE = 16
+OFFSETS = (1, 11, 2, 10, 3, 9, 4, 8, 5, 7, 6)
+
+
+def slab_order(fields, rows):
+    order = [(f, r) for r in range(1, rows - 1) for f in range(fields)]
+    return order + [(f, r) for r in (0, rows - 1) for f in range(fields)]
 
 
 def split_bf16(table):
@@ -162,9 +168,16 @@
     east = (lat, lax.rem(lon + 1, SECTORS))
     slot = jnp.where(chip < 3, 2 * chip, 11 - 2 * chip)
     starts = (
-        jnp.where(main, 2 * lon, 48 + 4 * slot + 2 * core),
-        jnp.where(main, 24 + 2 * lon, 72 + 3 * slot + 2 * core),
+        jnp.where(main, 24 + 2 * lon, 4 * slot + 2 * core),
+        jnp.where(main, 66 + 2 * lon, 48 + 3 * slot + 2 * core),
     )
+    order = slab_order(fields, rows)
+    half = STRIDE // 2
+    place = lax.rem(lat, STRIDE)
+    far_north = jnp.logical_and(lax.rem(place, half) == 0, jnp.logical_not(low_edge))
+    far_south = jnp.logical_and(lax.rem(place, half) == half - 1, jnp.logical_not(high_edge))
+    upper = place >= half
+    lower_far = jnp.logical_and(place < half, jnp.logical_or(far_north, far_south))
 
     def turned(offset):
         return lax.rem(lon + offset, SECTORS)
@@ -196,8 +209,12 @@
     ]
 
     barrier = pltpu.get_barrier_semaphore()
-    for target in (north, south, west, east):
-        greet(target)
+    greet(west)
+    greet(east)
+    for target, far in ((north, far_north), (south, far_south)):
+        @pl.when(jnp.logical_not(jnp.logical_and(upper, far)))
+        def _():
+            greet(target)
 
     @pl.when(jnp.logical_or(main, helper))
     def _():
@@ -241,17 +258,8 @@
             edge_out[side, f] = q_pad[f, row]
         edge_out[side, fields] = v_pad[row]
 
-    @pl.when(main)
-    def _():
-        pl.semaphore_wait(barrier, 4 + SECTORS - 3 + 1)
-
-    @pl.when(helper)
-    def _():
-        pl.semaphore_wait(barrier, 4 + SECTORS - 3 + SECTORS)
-
-    @pl.when(jnp.logical_not(jnp.logical_or(main, helper)))
-    def _():
-        pl.semaphore_wait(barrier, 4)
+    greeted = jnp.where(main, 4 + SECTORS - 3 + 1, jnp.where(helper, 4 + SECTORS - 3 + SECTORS, 4))
+    pl.semaphore_wait(barrier, greeted - jnp.where(lower_far, 1, 0))
 
     def edge_copy(side, slot, target):
         return pltpu.make_async_remote_copy(
@@ -273,8 +281,59 @@
         src_ref=side_out.at[1], dst_ref=side_in.at[0], send_sem=halo_send.at[3],
         recv_sem=halo_recv.at[3], device_id=east, device_id_type=MESH,
     )
-    for copy in (to_north, to_south, to_west, to_east):
-        copy.start()
+    to_west.start()
+    to_east.start()
+    for copy, far in ((to_north, far_north), (to_south, far_south)):
+        @pl.when(jnp.logical_or(upper, jnp.logical_not(far)))
+        def _():
+            copy.start()
+
+    def edges_arrive():
+        edge_copy(0, 0, north).wait_recv()
+        edge_copy(1, 1, south).wait_recv()
+        for copy, far in ((to_north, far_north), (to_south, far_south)):
+            @pl.when(jnp.logical_and(lower_far, far))
+            def _():
+                copy.start()
+
+    flip_north = jnp.where(low_edge, -1.0, 1.0)
+    flip_south = jnp.where(high_edge, -1.0, 1.0)
+
+    def step(slabs, winds):
+        from_west, from_east = side_in[0], side_in[1]
+
+        def with_ghosts(x, s):
+            x = jnp.where(lane == sector, pltpu.roll(from_east, (sector - s) % LANES, 1), x)
+            return jnp.where(lane == LANES - 1, pltpu.roll(from_west, (LANES - 1 - s) % LANES, 1), x)
+
+        for p in slabs:
+            f, r = order[p]
+            if r not in winds:
+                u = with_ghosts(u_pad[r], fields * rows + r)
+                v = v_pad[r]
+                v_next = v_pad[r + 1] if r < rows - 1 else edge_in[1, fields] * flip_south
+                v_previous = v_pad[r - 1] if r > 0 else edge_in[0, fields] * flip_north
+                speeds = (
+                    0.5 * (u + pltpu.roll(u, LANES - 1, 1)), 0.5 * (pltpu.roll(u, 1, 1) + u),
+                    0.5 * (v + v_next), 0.5 * (v_previous + v),
+                )
+                winds[r] = [(jnp.maximum(x, 0.0), jnp.minimum(x, 0.0)) for x in speeds]
+            (e_plus, e_minus), (w_plus, w_minus), (s_plus, s_minus), (n_plus, n_minus) = winds[r]
+            q = with_ghosts(q_pad[f, r], f * rows + r)
+            q_next = q_pad[f, r + 1] if r < rows - 1 else edge_in[1, f]
+            q_previous = q_pad[f, r - 1] if r > 0 else edge_in[0, f]
+            east_flux = e_plus * q + e_minus * pltpu.roll(q, LANES - 1, 1)
+            west_flux = w_plus * pltpu.roll(q, 1, 1) + w_minus * q
+            south_flux = s_plus * q + s_minus * q_next
+            north_flux = n_plus * q_previous + n_minus * q
+            new = q - (east_flux - west_flux) - (south_flux - north_flux)
+            new = jnp.where(lane < sector, new, 0.0)
+            stepped[2 * p] = new[:8]
+            stepped[2 * p + 1] = new[8:]
+
+    def hand_out(source):
+        for p, (f, r) in enumerate(order):
+            out_ref[pl.ds(2 * (f * rows + r), 2)] = source[pl.ds(2 * p, 2)]
 
     @pl.when(main)
     def _():
@@ -312,65 +371,39 @@
 
     to_west.wait_recv()
     to_east.wait_recv()
-    edge_copy(0, 0, north).wait_recv()
-    edge_copy(1, 1, south).wait_recv()
-
-    from_west, from_east = side_in[0], side_in[1]
-
-    def with_ghosts(x, s):
-        x = jnp.where(lane == sector, pltpu.roll(from_east, (sector - s) % LANES, 1), x)
-        return jnp.where(lane == LANES - 1, pltpu.roll(from_west, (LANES - 1 - s) % LANES, 1), x)
-
-    flip_north = jnp.where(low_edge, -1.0, 1.0)
-    flip_south = jnp.where(high_edge, -1.0, 1.0)
-    for r in range(rows):
-        u = with_ghosts(u_pad[r], fields * rows + r)
-        east_speed = 0.5 * (u + pltpu.roll(u, LANES - 1, 1))
-        west_speed = 0.5 * (pltpu.roll(u, 1, 1) + u)
-        v = v_pad[r]
-        v_next = v_pad[r + 1] if r < rows - 1 else edge_in[1, fields] * flip_south
-        v_previous = v_pad[r - 1] if r > 0 else edge_in[0, fields] * flip_north
-        south_speed = 0.5 * (v + v_next)
-        north_speed = 0.5 * (v_previous + v)
-        e_plus, e_minus = jnp.maximum(east_speed, 0.0), jnp.minimum(east_speed, 0.0)
-        w_plus, w_minus = jnp.maximum(west_speed, 0.0), jnp.minimum(west_speed, 0.0)
-        s_plus, s_minus = jnp.maximum(south_speed, 0.0), jnp.minimum(south_speed, 0.0)
-        n_plus, n_minus = jnp.maximum(north_speed, 0.0), jnp.minimum(north_speed, 0.0)
-        for f in range(fields):
-            q = with_ghosts(q_pad[f, r], f * rows + r)
-            q_next = q_pad[f, r + 1] if r < rows - 1 else edge_in[1, f]
-            q_previous = q_pad[f, r - 1] if r > 0 else edge_in[0, f]
-            east_flux = e_plus * q + e_minus * pltpu.roll(q, LANES - 1, 1)
-            west_flux = w_plus * pltpu.roll(q, 1, 1) + w_minus * q
-            south_flux = s_plus * q + s_minus * q_next
-            north_flux = n_plus * q_previous + n_minus * q
-            new = q - (east_flux - west_flux) - (south_flux - north_flux)
-            new = jnp.where(lane < sector, new, 0.0)
-            tile = 2 * (f * rows + r)
-            stepped[tile] = new[:8]
-            stepped[tile + 1] = new[8:]
-
-    @pl.when(jnp.logical_not(main))
-    def _():
-        out_ref[...] = stepped[...]
 
     @pl.when(main)
     def _():
-        for phase in range(2):
+        winds = {}
+
+        def for_helper(phase):
             for group in range(3):
                 count = (8, 6)[phase]
-                at = 24 * phase + count * group
+                at = 48 * phase + count * group
+                step(range(at // 2, (at + count) // 2), winds)
                 send(
-                    stepped.at[pl.ds(48 + at, count)], relay.at[pl.ds(at, count)],
+                    stepped.at[pl.ds(at, count)], relay.at[pl.ds(24 * phase + count * group, count)],
                     relay_send, relay_recv.at[3 * phase + group], (mate, lon),
                 )
-            for offset in range(1, SECTORS):
+
+        def for_line(phase):
+            at = (24, 66)[phase]
+            for offset in OFFSETS:
                 to = turned(offset)
                 send(
-                    stepped.at[pl.ds(24 * phase + 2 * to, 2)], land.at[lon, pl.ds(2 * phase, 2)],
+                    stepped.at[pl.ds(at + 2 * to, 2)], land.at[lon, pl.ds(2 * phase, 2)],
                     go_send.at[phase], go_recv.at[phase], (lat, to),
                 )
-            land[lon, pl.ds(2 * phase, 2)] = stepped[pl.ds(24 * phase + 2 * lon, 2)]
+            land[lon, pl.ds(2 * phase, 2)] = stepped[pl.ds(at + 2 * lon, 2)]
+
+        for_helper(0)
+        step(range(12, 24), winds)
+        for_line(0)
+        for_helper(1)
+        step(range(33, 35), winds)
+        edges_arrive()
+        step(range(35, 45), winds)
+        for_line(1)
 
     @pl.when(helper)
     def _():
@@ -390,7 +423,9 @@
             x = [land[j, pl.ds(2 * phase, 2)].reshape(16, LANES) for j in range(SECTORS)]
             limits = []
             for i in range(2):
-                row = lax.rem((starts[phase] + i) // 2, rows)
+                p = (starts[phase] + i) // 2
+                row = 1 + p // fields
+                row = jnp.where(p < fields * (rows - 1), jnp.where(row < rows - 1, row, 0), rows - 1)
                 limit = jnp.broadcast_to(cut_rows[pl.ds(row, 1)], (8, LANES))
                 limits.append(jnp.concatenate([limit, limit], axis=1))
             limits = jnp.concatenate(limits, axis=0)
@@ -412,7 +447,7 @@
                             back_send.at[phase], back_recv.at[phase], (team, to),
                         )
 
-                    for offset in range(1, SECTORS):
+                    for offset in OFFSETS:
                         back(turned(offset))
 
                     @pl.when(helper)
@@ -427,7 +462,7 @@
     def _():
         waiter(result.at[pl.ds(0, 46)], back_recv.at[0]).wait()
         waiter(result.at[pl.ds(0, 40)], back_recv.at[1]).wait()
-        out_ref[...] = result[...]
+        hand_out(result)
         for phase in range(2):
             waiter(stepped.at[pl.ds(0, 22)], go_send.at[phase]).wait()
             waiter(stepped.at[pl.ds(0, 22)], back_send.at[phase]).wait()
@@ -443,6 +478,12 @@
             def _():
                 waiter(stepped.at[pl.ds(0, 16 + c)], go_send.at[1]).wait()
                 waiter(stepped.at[pl.ds(0, 24 - 12 * c)], back_send.at[1]).wait()
+
+    @pl.when(jnp.logical_not(main))
+    def _():
+        edges_arrive()
+        step(range(len(order)), {})
+        hand_out(stepped)
 
     for copy in (to_north, to_south, to_west, to_east):
         copy.wait_send()

time: 45.4 us -> 41.5 us (0.914)
  the two profiles are of different devices: /device:TPU:63 before, /device:TPU:1 now
where the time goes in v4:
time: 41.5 us; the launch traced here: 41.3 us
  Pallas kernels  39.6 us (95%)
  local copies, waits for them, and re-layouts  1.75 us (4%)
    pallas_call x1, Pallas kernels, body(): pl.pallas_call(functools.partial(kernel, lat_count, fields, rows), out_sh...  39.6 us
    transpose x1, local copies, waits for them, and re-layouts, body(): return jnp.transpose(out, (0, 2, 1, 3))  1.75 us

profile of v4, /device:TPU:1, one launch (start us, length us, event | category | flops | bytes accessed | tf_op | source)
XLA Modules:
  0.0 41.3 jit_solution(6504865966400136315)
XLA Ops:
  0.0 39.6 %shard_map.91 = f32[90,8,128]{2,1,0:T(8,128)} custom-call(f32[5,9,16,120]{3,2,1,0:T(8,128)} %bitcast.7, f32[9,16,120]{2,1,0:T(8,128)} %bitcast.8, f32[9,16,120]{2,1,0:T(8,128)} %bitcast.9, s32[9]{0:T(128)} %cut_hbm.1, bf16[6,256,256]{2,1,0:T(8,128)(2,1)} %constant.10.clone.fh_hbm, bf16[6,256,256]{2,1,0:T(8,128)(2,1)} %constant.11.clone.fl_hbm, ...), custom_call_target="tpu_custom_call" | custom-call | tf_op jit(solution)/shard_map/pallas_call | solution.py:503
  39.6 1.7 %slice_bitcast_fusion = f32[5,16,9,120]{3,1,2,0:T(8,128)} fusion(f32[5,9,16,128]{3,2,1,0:T(8,128)} %bitcast.6), kind=kLoop, calls=%fused_computation | loop fusion | bytes 691200 | tf_op jit(solution)/shard_map/transpose | solution.py:540

commit v5 on v4

--- a/solution.py
+++ b/solution.py
@@ -144,7 +144,7 @@
     out_ref,
     q_in, u_in, v_in, q_pad, u_pad, v_pad, edge_out, edge_in, side_out, side_in,
     fh, fl, ih, il, waves_ref, cut_ref, cut_out, cut_rows, stepped, relay, land, done, result,
-    load_sem, table_sem, halo_send, halo_recv, cut_send, cut_recv, relay_send, relay_recv,
+    load_sem, table_sem, halo_send, halo_recv, cut_send, cut_recv, relay_send, relay_recv, hello,
     go_send, go_recv, back_send, back_recv,
 ):
     lat, lon = lax.axis_index("lat"), lax.axis_index("lon")
@@ -166,18 +166,29 @@
     south = (jnp.where(high_edge, lat, lat + 1), jnp.where(high_edge, across, lon))
     west = (lat, lax.rem(lon + SECTORS - 1, SECTORS))
     east = (lat, lax.rem(lon + 1, SECTORS))
-    slot = jnp.where(chip < 3, 2 * chip, 11 - 2 * chip)
     starts = (
-        jnp.where(main, 24 + 2 * lon, 4 * slot + 2 * core),
-        jnp.where(main, 66 + 2 * lon, 48 + 3 * slot + 2 * core),
+        jnp.where(main, 24 + 2 * lon, 2 * lon),
+        jnp.where(main, 66 + 2 * lon, 48 + 3 * chip + 2 * core),
     )
+    first = jnp.where(low_edge, 1, 0)
+    rank = lax.rem(lon + SECTORS - first, SECTORS)
     order = slab_order(fields, rows)
     half = STRIDE // 2
     place = lax.rem(lat, STRIDE)
     far_north = jnp.logical_and(lax.rem(place, half) == 0, jnp.logical_not(low_edge))
     far_south = jnp.logical_and(lax.rem(place, half) == half - 1, jnp.logical_not(high_edge))
     upper = place >= half
-    lower_far = jnp.logical_and(place < half, jnp.logical_or(far_north, far_south))
+    north_late = jnp.logical_or(
+        jnp.logical_and(far_north, jnp.logical_not(upper)), jnp.logical_and(lat == 1, lon == 0)
+    )
+    south_late = jnp.logical_and(far_south, jnp.logical_not(upper))
+    late_for_north = jnp.logical_and(far_north, upper)
+    late_for_south = jnp.logical_or(
+        jnp.logical_and(far_south, upper), jnp.logical_and(low_edge, lon == 0)
+    )
+
+    def ranked(t):
+        return lax.rem(t + first, SECTORS)
 
     def turned(offset):
         return lax.rem(lon + offset, SECTORS)
@@ -209,31 +220,50 @@
     ]
 
     barrier = pltpu.get_barrier_semaphore()
-    greet(west)
-    greet(east)
-    for target, far in ((north, far_north), (south, far_south)):
-        @pl.when(jnp.logical_not(jnp.logical_and(upper, far)))
+    for target, pole, late in ((north, low_edge, late_for_north), (south, high_edge, late_for_south)):
+        @pl.when(jnp.logical_not(jnp.logical_or(pole, late)))
         def _():
             greet(target)
 
-    @pl.when(jnp.logical_or(main, helper))
-    def _():
-        for offset in range(2, SECTORS - 1):
-            greet((lat, turned(offset)))
+    team_member = jnp.logical_or(main, helper)
+
+    @pl.when(team_member)
+    def _():
+        for t in range(1, SECTORS):
+            @pl.when(t > rank)
+            def _():
+                greet((lat, ranked(t)))
+
+    @pl.when(jnp.logical_not(team_member))
+    def _():
+        greet(west)
+        greet(east)
+
+    @pl.when(helper)
+    def _():
+        greet((mate, lon))
+
+    greeted = jnp.where(main, rank + 1, jnp.where(helper, rank, 2))
+    for pole, late in ((low_edge, north_late), (high_edge, south_late)):
+        greeted += jnp.where(jnp.logical_or(pole, late), 0, 1)
+    pl.semaphore_wait(barrier, greeted)
+
+    @pl.when(team_member)
+    def _():
+        for t in range(SECTORS - 1):
+            @pl.when(t < rank)
+            def _():
+                pl.semaphore_signal(
+                    hello.at[rank], inc=1, device_id=(lat, ranked(t)), device_id_type=MESH
+                )
+
+    for load in loads:
+        load.wait()
+
+    @pl.when(team_member)
+    def _():
         for table in tables:
             table.start()
-
-    @pl.when(main)
-    def _():
-        for offset in range(SECTORS):
-            greet((mate, turned(offset)))
-
-    @pl.when(helper)
-    def _():
-        greet((mate, lon))
-
-    for load in loads:
-        load.wait()
 
     sector = q_in.shape[-1]
     lane = lax.broadcasted_iota(jnp.int32, (16, LANES), 1)
@@ -258,9 +288,6 @@
             edge_out[side, f] = q_pad[f, row]
         edge_out[side, fields] = v_pad[row]
 
-    greeted = jnp.where(main, 4 + SECTORS - 3 + 1, jnp.where(helper, 4 + SECTORS - 3 + SECTORS, 4))
-    pl.semaphore_wait(barrier, greeted - jnp.where(lower_far, 1, 0))
-
     def edge_copy(side, slot, target):
         return pltpu.make_async_remote_copy(
             src_ref=edge_out.at[side],
@@ -281,35 +308,65 @@
         src_ref=side_out.at[1], dst_ref=side_in.at[0], send_sem=halo_send.at[3],
         recv_sem=halo_recv.at[3], device_id=east, device_id_type=MESH,
     )
-    to_west.start()
-    to_east.start()
-    for copy, far in ((to_north, far_north), (to_south, far_south)):
-        @pl.when(jnp.logical_or(upper, jnp.logical_not(far)))
+    for copy, pole, late in ((to_north, low_edge, north_late), (to_south, high_edge, south_late)):
+        @pl.when(jnp.logical_not(jnp.logical_or(pole, late)))
         def _():
             copy.start()
+
+    @pl.when(jnp.logical_not(team_member))
+    def _():
+        to_west.start()
+        to_east.start()
+
+    @pl.when(main)
+    def _():
+        @pl.when(rank > 0)
+        def _():
+            to_west.start()
+
+        @pl.when(rank < SECTORS - 1)
+        def _():
+            pl.semaphore_wait(hello.at[rank + 1], 1)
+
+        to_east.start()
+
+        @pl.when(rank == 0)
+        def _():
+            pl.semaphore_wait(hello.at[SECTORS - 1], 1)
+            to_west.start()
 
     def edges_arrive():
         edge_copy(0, 0, north).wait_recv()
         edge_copy(1, 1, south).wait_recv()
-        for copy, far in ((to_north, far_north), (to_south, far_south)):
-            @pl.when(jnp.logical_and(lower_far, far))
+        for copy, late in ((to_north, north_late), (to_south, south_late)):
+            @pl.when(late)
             def _():
                 copy.start()
 
+    ghosts = set()
     flip_north = jnp.where(low_edge, -1.0, 1.0)
     flip_south = jnp.where(high_edge, -1.0, 1.0)
 
+    def set_ghosts(slabs):
+        from_west, from_east = side_in[0], side_in[1]
+        wanted = []
+        for p in slabs:
+            f, r = order[p]
+            if (fields, r) not in ghosts:
+                wanted.append((fields, r))
+                ghosts.add((fields, r))
+            wanted.append((f, r))
+        for f, r in wanted:
+            s = f * rows + r
+            pad = q_pad.at[f] if f < fields else u_pad
+            x = jnp.where(lane == sector, pltpu.roll(from_east, (sector - s) % LANES, 1), pad[r])
+            pad[r] = jnp.where(lane == LANES - 1, pltpu.roll(from_west, (LANES - 1 - s) % LANES, 1), x)
+
     def step(slabs, winds):
-        from_west, from_east = side_in[0], side_in[1]
-
-        def with_ghosts(x, s):
-            x = jnp.where(lane == sector, pltpu.roll(from_east, (sector - s) % LANES, 1), x)
-            return jnp.where(lane == LANES - 1, pltpu.roll(from_west, (LANES - 1 - s) % LANES, 1), x)
-
         for p in slabs:
             f, r = order[p]
             if r not in winds:
-                u = with_ghosts(u_pad[r], fields * rows + r)
+                u = u_pad[r]
                 v = v_pad[r]
                 v_next = v_pad[r + 1] if r < rows - 1 else edge_in[1, fields] * flip_south
                 v_previous = v_pad[r - 1] if r > 0 else edge_in[0, fields] * flip_north
@@ -319,7 +376,7 @@
                 )
                 winds[r] = [(jnp.maximum(x, 0.0), jnp.minimum(x, 0.0)) for x in speeds]
             (e_plus, e_minus), (w_plus, w_minus), (s_plus, s_minus), (n_plus, n_minus) = winds[r]
-            q = with_ghosts(q_pad[f, r], f * rows + r)
+            q = q_pad[f, r]
             q_next = q_pad[f, r + 1] if r < rows - 1 else edge_in[1, f]
             q_previous = q_pad[f, r - 1] if r > 0 else edge_in[0, f]
             east_flux = e_plus * q + e_minus * pltpu.roll(q, LANES - 1, 1)
@@ -352,29 +409,39 @@
                 count = (8, 6)[phase]
                 chunk = relay.at[pl.ds(24 * phase + count * group, count)]
                 waiter(chunk, relay_recv.at[3 * phase + group]).wait()
-                for place, to_chip in enumerate((group, 5 - group)):
-                    for c in range(2):
-                        to = 2 * to_chip + c
-                        n = 2 - phase * c
-                        at = 24 * phase + count * group + count // 2 * place + 2 * c
-
-                        @pl.when(lon != to)
+                for to in range(4 * group, 4 * group + 4):
+                    c = to % 2
+                    n = 2 - phase * c
+                    at = 24 * phase + count * group + count // 2 * (to // 2 % 2) + 2 * c
+
+                    if phase == 0:
+                        @pl.when(to > rank)
                         def _():
-                            send(
-                                relay.at[pl.ds(at, n)], land.at[lon, pl.ds(2 * phase, n)],
-                                go_send.at[phase], go_recv.at[phase], (lat, to),
-                            )
-
-                        @pl.when(lon == to)
-                        def _():
-                            land[lon, pl.ds(2 * phase, n)] = relay[pl.ds(at, n)]
-
-    to_west.wait_recv()
-    to_east.wait_recv()
+                            pl.semaphore_wait(hello.at[to], 1)
+
+                    @pl.when(lon != to)
+                    def _():
+                        send(
+                            relay.at[pl.ds(at, n)], land.at[lon, pl.ds(2 * phase, n)],
+                            go_send.at[phase], go_recv.at[phase], (lat, to),
+                        )
+
+                    @pl.when(lon == to)
+                    def _():
+                        land[lon, pl.ds(2 * phase, n)] = relay[pl.ds(at, n)]
+
+        to_west.start()
+        to_east.start()
+
+    def sides_arrive():
+        to_west.wait_recv()
+        to_east.wait_recv()
 
     @pl.when(main)
     def _():
         winds = {}
+        ghosts.clear()
+        sides_arrive()
 
         def for_helper(phase):
             for group in range(3):
@@ -388,17 +455,31 @@
 
         def for_line(phase):
             at = (24, 66)[phase]
-            for offset in OFFSETS:
-                to = turned(offset)
-                send(
-                    stepped.at[pl.ds(at + 2 * to, 2)], land.at[lon, pl.ds(2 * phase, 2)],
-                    go_send.at[phase], go_recv.at[phase], (lat, to),
-                )
+            for t in range(SECTORS):
+                to = ranked(t)
+                if phase == 0:
+                    @pl.when(jnp.logical_and(t > rank + 1, jnp.logical_or(rank > 0, t < SECTORS - 1)))
+                    def _():
+                        pl.semaphore_wait(hello.at[t], 1)
+
+                @pl.when(t != rank)
+                def _():
+                    send(
+                        stepped.at[pl.ds(at + 2 * to, 2)], land.at[lon, pl.ds(2 * phase, 2)],
+                        go_send.at[phase], go_recv.at[phase], (lat, to),
+                    )
             land[lon, pl.ds(2 * phase, 2)] = stepped[pl.ds(at + 2 * lon, 2)]
 
+        set_ghosts(range(24))
         for_helper(0)
         step(range(12, 24), winds)
         for_line(0)
+        for copy, pole in ((to_north, low_edge), (to_south, high_edge)):
+            @pl.when(pole)
+            def _():
+                copy.start()
+
+        set_ghosts(range(24, 45))
         for_helper(1)
         step(range(33, 35), winds)
         edges_arrive()
@@ -481,6 +562,9 @@
 
     @pl.when(jnp.logical_not(main))
     def _():
+        ghosts.clear()
+        sides_arrive()
+        set_ghosts(range(len(order)))
         edges_arrive()
         step(range(len(order)), {})
         hand_out(stepped)
@@ -529,7 +613,7 @@
             pltpu.VMEM((SECTORS, 4, 8, LANES), f32),
             pltpu.VMEM((SECTORS, 4, 8, LANES), f32),
             pltpu.VMEM((tiles, 8, LANES), f32),
-            dma((3,)), dma((6,)), dma((4,)), dma((4,)), dma, dma, dma, dma((6,)),
+            dma((3,)), dma((6,)), dma((4,)), dma((4,)), dma, dma, dma, dma((6,)), pltpu.SemaphoreType.REGULAR((SECTORS,)),
             dma((2,)), dma((2,)), dma((2,)), dma((2,)),
         ],
         compiler_params=pltpu.CompilerParams(

time: 41.5 us -> 42.7 us (1.029)
  Pallas kernels: 39.6 us -> 40.8 us
    pallas_call x1, Pallas kernels: 39.6 us -> 40.8 us  [body(): pl.pallas_call(functools.partial(kernel, lat_count, fields, rows), out_sh...]
where the time goes in v5:
time: 42.7 us; the launch traced here: 42.6 us
  Pallas kernels  40.8 us (96%)
  local copies, waits for them, and re-layouts  1.75 us (4%)
    pallas_call x1, Pallas kernels, body(): pl.pallas_call(functools.partial(kernel, lat_count, fields, rows), out_sh...  40.8 us
    transpose x1, local copies, waits for them, and re-layouts, body(): return jnp.transpose(out, (0, 2, 1, 3))  1.75 us

profile of v5, /device:TPU:1, one launch (start us, length us, event | category | flops | bytes accessed | tf_op | source)
XLA Modules:
  0.0 42.6 jit_solution(2954586880736129632)
XLA Ops:
  0.0 40.8 %shard_map.91 = f32[90,8,128]{2,1,0:T(8,128)} custom-call(f32[5,9,16,120]{3,2,1,0:T(8,128)} %bitcast.7, f32[9,16,120]{2,1,0:T(8,128)} %bitcast.8, f32[9,16,120]{2,1,0:T(8,128)} %bitcast.9, s32[9]{0:T(128)} %cut_hbm.1, bf16[6,256,256]{2,1,0:T(8,128)(2,1)} %constant.10.clone.fh_hbm, bf16[6,256,256]{2,1,0:T(8,128)(2,1)} %constant.11.clone.fl_hbm, ...), custom_call_target="tpu_custom_call" | custom-call | tf_op jit(solution)/shard_map/pallas_call | solution.py:587
  40.8 1.7 %slice_bitcast_fusion = f32[5,16,9,120]{3,1,2,0:T(8,128)} fusion(f32[5,9,16,128]{3,2,1,0:T(8,128)} %bitcast.6), kind=kLoop, calls=%fused_computation | loop fusion | bytes 691200 | tf_op jit(solution)/shard_map/transpose | solution.py:624

commit v6 on v5

--- a/solution.py
+++ b/solution.py
@@ -172,6 +172,7 @@
     )
     first = jnp.where(low_edge, 1, 0)
     rank = lax.rem(lon + SECTORS - first, SECTORS)
+    eager = lax.rem(lat, STRIDE) < STRIDE // 2
     order = slab_order(fields, rows)
     half = STRIDE // 2
     place = lax.rem(lat, STRIDE)
@@ -229,8 +230,8 @@
 
     @pl.when(team_member)
     def _():
-        for t in range(1, SECTORS):
-            @pl.when(t > rank)
+        for t in range(SECTORS):
+            @pl.when(jnp.logical_or(t > rank, jnp.logical_and(t < rank, jnp.logical_not(eager))))
             def _():
                 greet((lat, ranked(t)))
 
@@ -243,7 +244,8 @@
     def _():
         greet((mate, lon))
 
-    greeted = jnp.where(main, rank + 1, jnp.where(helper, rank, 2))
+    seen = jnp.where(eager, rank, SECTORS - 1)
+    greeted = jnp.where(main, seen + 1, jnp.where(helper, seen, 2))
     for pole, late in ((low_edge, north_late), (high_edge, south_late)):
         greeted += jnp.where(jnp.logical_or(pole, late), 0, 1)
     pl.semaphore_wait(barrier, greeted)
@@ -251,7 +253,7 @@
     @pl.when(team_member)
     def _():
         for t in range(SECTORS - 1):
-            @pl.when(t < rank)
+            @pl.when(jnp.logical_and(t < rank, eager))
             def _():
                 pl.semaphore_signal(
                     hello.at[rank], inc=1, device_id=(lat, ranked(t)), device_id_type=MESH
@@ -324,7 +326,7 @@
         def _():
             to_west.start()
 
-        @pl.when(rank < SECTORS - 1)
+        @pl.when(jnp.logical_and(rank < SECTORS - 1, eager))
         def _():
             pl.semaphore_wait(hello.at[rank + 1], 1)
 
@@ -332,7 +334,10 @@
 
         @pl.when(rank == 0)
         def _():
-            pl.semaphore_wait(hello.at[SECTORS - 1], 1)
+            @pl.when(eager)
+            def _():
+                pl.semaphore_wait(hello.at[SECTORS - 1], 1)
+
             to_west.start()
 
     def edges_arrive():
@@ -390,7 +395,7 @@
 
     def hand_out(source):
         for p, (f, r) in enumerate(order):
-            out_ref[pl.ds(2 * (f * rows + r), 2)] = source[pl.ds(2 * p, 2)]
+            out_ref[f, r] = source[pl.ds(2 * p, 2)].reshape(16, LANES)[:, :sector]
 
     @pl.when(main)
     def _():
@@ -415,7 +420,7 @@
                     at = 24 * phase + count * group + count // 2 * (to // 2 % 2) + 2 * c
 
                     if phase == 0:
-                        @pl.when(to > rank)
+                        @pl.when(jnp.logical_and(to > rank, eager))
                         def _():
                             pl.semaphore_wait(hello.at[to], 1)
 
@@ -458,9 +463,16 @@
             for t in range(SECTORS):
                 to = ranked(t)
                 if phase == 0:
-                    @pl.when(jnp.logical_and(t > rank + 1, jnp.logical_or(rank > 0, t < SECTORS - 1)))
+                    waits = jnp.logical_and(t > rank + 1, jnp.logical_or(rank > 0, t < SECTORS - 1))
+
+                    @pl.when(jnp.logical_and(waits, eager))
                     def _():
                         pl.semaphore_wait(hello.at[t], 1)
+
+                    for copy, pole in ((to_north, low_edge), (to_south, high_edge)):
+                        @pl.when(jnp.logical_and(pole, to == across))
+                        def _():
+                            copy.start()
 
                 @pl.when(t != rank)
                 def _():
@@ -474,11 +486,6 @@
         for_helper(0)
         step(range(12, 24), winds)
         for_line(0)
-        for copy, pole in ((to_north, low_edge), (to_south, high_edge)):
-            @pl.when(pole)
-            def _():
-                copy.start()
-
         set_ghosts(range(24, 45))
         for_helper(1)
         step(range(33, 35), winds)
@@ -586,7 +593,7 @@
     vmem = pl.BlockSpec(memory_space=pltpu.VMEM)
     out = pl.pallas_call(
         functools.partial(kernel, lat_count, fields, rows),
-        out_shape=jax.ShapeDtypeStruct((tiles, 8, LANES), f32),
+        out_shape=jax.ShapeDtypeStruct((fields, rows, levels, sector), f32),
         in_specs=[hbm] * 9,
         out_specs=vmem,
         scratch_shapes=[
@@ -620,7 +627,6 @@
             collective_id=0, has_side_effects=True, vmem_limit_bytes=60 * 1024 * 1024
         ),
     )(q, u, v, cutoff, *tables)
-    out = out.reshape(fields, rows, levels, LANES)[..., :sector]
     return jnp.transpose(out, (0, 2, 1, 3))
 
 

time: 42.7 us -> 42.9 us (level)
    transpose x1 -> x0, local copies, waits for them, and re-layouts: 1.75 us -> none  [body(): return jnp.transpose(out, (0, 2, 1, 3))]
    unnamed x0 -> x1, local copies, waits for them, and re-layouts: none -> 1.75 us
where the time goes in v6:
time: 42.9 us; the launch traced here: 42.7 us
  Pallas kernels  40.9 us (95%)
  local copies, waits for them, and re-layouts  1.75 us (4%)
    pallas_call x1, Pallas kernels, body(): pl.pallas_call(functools.partial(kernel, lat_count, fields, rows), out_sh...  40.9 us
    unnamed x1, local copies, waits for them, and re-layouts  1.75 us

profile of v6, /device:TPU:1, one launch (start us, length us, event | category | flops | bytes accessed | tf_op | source)
XLA Modules:
  0.0 42.7 jit_solution(7180774056055500524)
XLA Ops:
  0.0 40.9 %shard_map.91 = f32[5,9,16,120]{3,2,1,0:T(8,128)} custom-call(f32[5,9,16,120]{3,2,1,0:T(8,128)} %bitcast.5, f32[9,16,120]{2,1,0:T(8,128)} %bitcast.6, f32[9,16,120]{2,1,0:T(8,128)} %bitcast.7, s32[9]{0:T(128)} %cut_hbm.1, bf16[6,256,256]{2,1,0:T(8,128)(2,1)} %constant.10.clone.fh_hbm, bf16[6,256,256]{2,1,0:T(8,128)(2,1)} %constant.11.clone.fl_hbm, ...), custom_call_target="tpu_custom_call" | custom-call | tf_op jit(solution)/shard_map/pallas_call | solution.py:594
  40.9 1.7 %copy.11 = f32[5,16,9,120]{3,1,2,0:T(8,128)} copy(f32[5,16,9,120]{3,1,2,0:T(8,128)} %bitcast.4) | data formatting | bytes 691200

commit v7 on v6

--- a/solution.py
+++ b/solution.py
@@ -166,19 +166,21 @@
     south = (jnp.where(high_edge, lat, lat + 1), jnp.where(high_edge, across, lon))
     west = (lat, lax.rem(lon + SECTORS - 1, SECTORS))
     east = (lat, lax.rem(lon + 1, SECTORS))
-    starts = (
-        jnp.where(main, 24 + 2 * lon, 2 * lon),
-        jnp.where(main, 66 + 2 * lon, 48 + 3 * chip + 2 * core),
-    )
     first = jnp.where(low_edge, 1, 0)
     rank = lax.rem(lon + SECTORS - first, SECTORS)
     eager = lax.rem(lat, STRIDE) < STRIDE // 2
+    inwards = jnp.where(chip < 3, 2 * chip, 11 - 2 * chip)
+    slot = jnp.where(eager, chip, inwards)
+    starts = (
+        jnp.where(main, 24 + 2 * lon, 4 * slot + 2 * core),
+        jnp.where(main, 66 + 2 * lon, 48 + 3 * inwards + 2 * core),
+    )
     order = slab_order(fields, rows)
     half = STRIDE // 2
-    place = lax.rem(lat, STRIDE)
-    far_north = jnp.logical_and(lax.rem(place, half) == 0, jnp.logical_not(low_edge))
-    far_south = jnp.logical_and(lax.rem(place, half) == half - 1, jnp.logical_not(high_edge))
-    upper = place >= half
+    place_in_run = lax.rem(lat, STRIDE)
+    far_north = jnp.logical_and(lax.rem(place_in_run, half) == 0, jnp.logical_not(low_edge))
+    far_south = jnp.logical_and(lax.rem(place_in_run, half) == half - 1, jnp.logical_not(high_edge))
+    upper = place_in_run >= half
     north_late = jnp.logical_or(
         jnp.logical_and(far_north, jnp.logical_not(upper)), jnp.logical_and(lat == 1, lon == 0)
     )
@@ -414,10 +416,12 @@
                 count = (8, 6)[phase]
                 chunk = relay.at[pl.ds(24 * phase + count * group, count)]
                 waiter(chunk, relay_recv.at[3 * phase + group]).wait()
-                for to in range(4 * group, 4 * group + 4):
-                    c = to % 2
+                for place, c in ((0, 0), (0, 1), (1, 0), (1, 1)):
+                    to = 2 * (5 - group if place else group) + c
+                    if phase == 0:
+                        to = jnp.where(eager, 2 * (2 * group + place) + c, to)
                     n = 2 - phase * c
-                    at = 24 * phase + count * group + count // 2 * (to // 2 % 2) + 2 * c
+                    at = 24 * phase + count * group + count // 2 * place + 2 * c
 
                     if phase == 0:
                         @pl.when(jnp.logical_and(to > rank, eager))
@@ -460,9 +464,10 @@
 
         def for_line(phase):
             at = (24, 66)[phase]
-            for t in range(SECTORS):
-                to = ranked(t)
+            for t, offset in enumerate((0,) + OFFSETS):
+                to = turned(offset)
                 if phase == 0:
+                    to = jnp.where(eager, ranked(t), to)
                     waits = jnp.logical_and(t > rank + 1, jnp.logical_or(rank > 0, t < SECTORS - 1))
 
                     @pl.when(jnp.logical_and(waits, eager))
@@ -474,7 +479,7 @@
                         def _():
                             copy.start()
 
-                @pl.when(t != rank)
+                @pl.when(to != lon)
                 def _():
                     send(
                         stepped.at[pl.ds(at + 2 * to, 2)], land.at[lon, pl.ds(2 * phase, 2)],

time: 42.9 us -> 42.9 us (level)
  no operation moved by 1% of the time
where the time goes in v7:
time: 42.9 us; the launch traced here: 42.7 us
  Pallas kernels  40.9 us (95%)
  local copies, waits for them, and re-layouts  1.75 us (4%)
    pallas_call x1, Pallas kernels, body(): pl.pallas_call(functools.partial(kernel, lat_count, fields, rows), out_sh...  40.9 us
    unnamed x1, local copies, waits for them, and re-layouts  1.75 us

profile of v7, /device:TPU:1, one launch (start us, length us, event | category | flops | bytes accessed | tf_op | source)
XLA Modules:
  0.0 42.7 jit_solution(3474617725352826276)
XLA Ops:
  0.0 40.9 %shard_map.91 = f32[5,9,16,120]{3,2,1,0:T(8,128)} custom-call(f32[5,9,16,120]{3,2,1,0:T(8,128)} %bitcast.5, f32[9,16,120]{2,1,0:T(8,128)} %bitcast.6, f32[9,16,120]{2,1,0:T(8,128)} %bitcast.7, s32[9]{0:T(128)} %cut_hbm.1, bf16[6,256,256]{2,1,0:T(8,128)(2,1)} %constant.10.clone.fh_hbm, bf16[6,256,256]{2,1,0:T(8,128)(2,1)} %constant.11.clone.fl_hbm, ...), custom_call_target="tpu_custom_call" | custom-call | tf_op jit(solution)/shard_map/pallas_call | solution.py:599
  40.9 1.7 %copy.11 = f32[5,16,9,120]{3,1,2,0:T(8,128)} copy(f32[5,16,9,120]{3,1,2,0:T(8,128)} %bitcast.4) | data formatting | bytes 691200

commit v8 on v7

--- a/solution.py
+++ b/solution.py
@@ -142,9 +142,9 @@
     lat_count, fields, rows,
     q_hbm, u_hbm, v_hbm, cut_hbm, fh_hbm, fl_hbm, ih_hbm, il_hbm, waves_hbm,
     out_ref,
-    q_in, u_in, v_in, q_pad, u_pad, v_pad, edge_out, edge_in, side_out, side_in,
+    q_in, u_in, v_in, q_pad, u_pad, v_pad, edge_out, edge_in, side_out, side_in, kept,
     fh, fl, ih, il, waves_ref, cut_ref, cut_out, cut_rows, stepped, relay, land, done, result,
-    load_sem, table_sem, halo_send, halo_recv, cut_send, cut_recv, relay_send, relay_recv, hello,
+    load_sem, table_sem, halo_send, halo_recv, kept_recv, cut_send, cut_recv, relay_send, relay_recv, hello, far_hello,
     go_send, go_recv, back_send, back_recv,
 ):
     lat, lon = lax.axis_index("lat"), lax.axis_index("lon")
@@ -168,7 +168,7 @@
     east = (lat, lax.rem(lon + 1, SECTORS))
     first = jnp.where(low_edge, 1, 0)
     rank = lax.rem(lon + SECTORS - first, SECTORS)
-    eager = lax.rem(lat, STRIDE) < STRIDE // 2
+    eager = lat >= 0
     inwards = jnp.where(chip < 3, 2 * chip, 11 - 2 * chip)
     slot = jnp.where(eager, chip, inwards)
     starts = (
@@ -251,6 +251,11 @@
     for pole, late in ((low_edge, north_late), (high_edge, south_late)):
         greeted += jnp.where(jnp.logical_or(pole, late), 0, 1)
     pl.semaphore_wait(barrier, greeted)
+
+    for target, late in ((north, late_for_north), (south, late_for_south)):
+        @pl.when(late)
+        def _():
+            pl.semaphore_signal(far_hello, inc=1, device_id=target, device_id_type=MESH)
 
     @pl.when(team_member)
     def _():
@@ -322,40 +327,54 @@
         to_west.start()
         to_east.start()
 
+    keeps = jnp.logical_and(low_edge, main)
+    to_keeper = pltpu.make_async_remote_copy(
+        src_ref=side_out.at[1], dst_ref=kept, send_sem=halo_send.at[3],
+        recv_sem=kept_recv, device_id=(lat, 1), device_id_type=MESH,
+    )
+    from_keeper = pltpu.make_async_remote_copy(
+        src_ref=kept, dst_ref=side_in.at[0], send_sem=halo_send.at[2],
+        recv_sem=halo_recv.at[3], device_id=(lat, 0), device_id_type=MESH,
+    )
+
     @pl.when(main)
     def _():
-        @pl.when(rank > 0)
-        def _():
-            to_west.start()
-
-        @pl.when(jnp.logical_and(rank < SECTORS - 1, eager))
+        to_kept = jnp.logical_and(keeps, lon == SECTORS - 1)
+
+        @pl.when(jnp.logical_and(rank < SECTORS - 1, jnp.logical_not(to_kept)))
         def _():
             pl.semaphore_wait(hello.at[rank + 1], 1)
 
-        to_east.start()
-
-        @pl.when(rank == 0)
+        @pl.when(jnp.logical_not(to_kept))
         def _():
-            @pl.when(eager)
-            def _():
-                pl.semaphore_wait(hello.at[SECTORS - 1], 1)
-
-            to_west.start()
+            to_east.start()
+
+        @pl.when(to_kept)
+        def _():
+            to_keeper.start()
+
+        @pl.when(jnp.logical_and(keeps, lon == 1))
+        def _():
+            pl.semaphore_wait(hello.at[SECTORS - 1], 1)
+            to_keeper.wait_recv()
+            from_keeper.start()
 
     def edges_arrive():
-        edge_copy(0, 0, north).wait_recv()
-        edge_copy(1, 1, south).wait_recv()
         for copy, late in ((to_north, north_late), (to_south, south_late)):
             @pl.when(late)
             def _():
+                pl.semaphore_wait(far_hello, 1)
                 copy.start()
+
+        edge_copy(0, 0, north).wait_recv()
+        edge_copy(1, 1, south).wait_recv()
 
     ghosts = set()
     flip_north = jnp.where(low_edge, -1.0, 1.0)
     flip_south = jnp.where(high_edge, -1.0, 1.0)
 
-    def set_ghosts(slabs):
-        from_west, from_east = side_in[0], side_in[1]
+    def set_ghosts(slabs, both):
+        from_west = side_in[0]
         wanted = []
         for p in slabs:
             f, r = order[p]
@@ -366,10 +385,12 @@
         for f, r in wanted:
             s = f * rows + r
             pad = q_pad.at[f] if f < fields else u_pad
-            x = jnp.where(lane == sector, pltpu.roll(from_east, (sector - s) % LANES, 1), pad[r])
+            x = pad[r]
+            if both:
+                x = jnp.where(lane == sector, pltpu.roll(side_in[1], (sector - s) % LANES, 1), x)
             pad[r] = jnp.where(lane == LANES - 1, pltpu.roll(from_west, (LANES - 1 - s) % LANES, 1), x)
 
-    def step(slabs, winds):
+    def step(slabs, winds, whole=False):
         for p in slabs:
             f, r = order[p]
             if r not in winds:
@@ -390,8 +411,12 @@
             west_flux = w_plus * pltpu.roll(q, 1, 1) + w_minus * q
             south_flux = s_plus * q + s_minus * q_next
             north_flux = n_plus * q_previous + n_minus * q
+            rest = 0.0
+            if not whole:
+                east_flux = jnp.where(lane < sector - 1, east_flux, 0.0)
+                rest = jnp.where(lane == LANES - 1, pltpu.roll(west_flux, LANES - 1, 1), 0.0)
             new = q - (east_flux - west_flux) - (south_flux - north_flux)
-            new = jnp.where(lane < sector, new, 0.0)
+            new = jnp.where(lane < sector, new, rest)
             stepped[2 * p] = new[:8]
             stepped[2 * p + 1] = new[8:]
 
@@ -414,6 +439,8 @@
         for phase in range(2):
             for group in range(3):
                 count = (8, 6)[phase]
+                if phase == 1 and group == 0:
+                    waiter(stepped.at[pl.ds(0, 22)], go_send.at[0]).wait()
                 chunk = relay.at[pl.ds(24 * phase + count * group, count)]
                 waiter(chunk, relay_recv.at[3 * phase + group]).wait()
                 for place, c in ((0, 0), (0, 1), (1, 0), (1, 1)):
@@ -442,15 +469,11 @@
         to_west.start()
         to_east.start()
 
-    def sides_arrive():
-        to_west.wait_recv()
-        to_east.wait_recv()
-
     @pl.when(main)
     def _():
         winds = {}
         ghosts.clear()
-        sides_arrive()
+        to_east.wait_recv()
 
         def for_helper(phase):
             for group in range(3):
@@ -459,7 +482,7 @@
                 step(range(at // 2, (at + count) // 2), winds)
                 send(
                     stepped.at[pl.ds(at, count)], relay.at[pl.ds(24 * phase + count * group, count)],
-                    relay_send, relay_recv.at[3 * phase + group], (mate, lon),
+                    relay_send.at[phase], relay_recv.at[3 * phase + group], (mate, lon),
                 )
 
         def for_line(phase):
@@ -468,7 +491,10 @@
                 to = turned(offset)
                 if phase == 0:
                     to = jnp.where(eager, ranked(t), to)
-                    waits = jnp.logical_and(t > rank + 1, jnp.logical_or(rank > 0, t < SECTORS - 1))
+                    waits = t > rank + 1
+                    if t == SECTORS - 1:
+                        waits = jnp.logical_and(waits, jnp.logical_not(jnp.logical_and(keeps, lon == 1)))
+                        waits = jnp.logical_or(waits, jnp.logical_and(keeps, lon == SECTORS - 1))
 
                     @pl.when(jnp.logical_and(waits, eager))
                     def _():
@@ -487,15 +513,17 @@
                     )
             land[lon, pl.ds(2 * phase, 2)] = stepped[pl.ds(at + 2 * lon, 2)]
 
-        set_ghosts(range(24))
+        set_ghosts(range(24), False)
         for_helper(0)
         step(range(12, 24), winds)
         for_line(0)
-        set_ghosts(range(24, 45))
+        set_ghosts(range(24, 45), False)
+        waiter(stepped.at[pl.ds(0, 24)], relay_send.at[0]).wait()
         for_helper(1)
         step(range(33, 35), winds)
         edges_arrive()
         step(range(35, 45), winds)
+        waiter(stepped.at[pl.ds(0, 22)], go_send.at[0]).wait()
         for_line(1)
 
     @pl.when(helper)
@@ -514,6 +542,11 @@
                 def _():
                     waiter(land.at[pl.ds(0, 11), pl.ds(0, n)], go_recv.at[phase]).wait()
             x = [land[j, pl.ds(2 * phase, 2)].reshape(16, LANES) for j in range(SECTORS)]
+            x = [
+                jnp.where(lane < sector, x[j], 0.0)
+                - jnp.where(lane == sector - 1, pltpu.roll(x[(j + 1) % SECTORS], sector, 1), 0.0)
+                for j in range(SECTORS)
+            ]
             limits = []
             for i in range(2):
                 p = (starts[phase] + i) // 2
@@ -556,15 +589,14 @@
         waiter(result.at[pl.ds(0, 46)], back_recv.at[0]).wait()
         waiter(result.at[pl.ds(0, 40)], back_recv.at[1]).wait()
         hand_out(result)
+        waiter(stepped.at[pl.ds(0, 22)], go_send.at[1]).wait()
         for phase in range(2):
-            waiter(stepped.at[pl.ds(0, 22)], go_send.at[phase]).wait()
             waiter(stepped.at[pl.ds(0, 22)], back_send.at[phase]).wait()
-        waiter(stepped.at[pl.ds(0, 42)], relay_send).wait()
+        waiter(stepped.at[pl.ds(0, 18)], relay_send.at[1]).wait()
         waiter(cut_out, cut_send).wait()
 
     @pl.when(helper)
     def _():
-        waiter(stepped.at[pl.ds(0, 22)], go_send.at[0]).wait()
         waiter(stepped.at[pl.ds(0, 24)], back_send.at[0]).wait()
         for c in range(2):
             @pl.when(core == c)
@@ -575,14 +607,19 @@
     @pl.when(jnp.logical_not(main))
     def _():
         ghosts.clear()
-        sides_arrive()
-        set_ghosts(range(len(order)))
+        to_west.wait_recv()
+        to_east.wait_recv()
+        set_ghosts(range(len(order)), True)
         edges_arrive()
-        step(range(len(order)), {})
+        step(range(len(order)), {}, True)
         hand_out(stepped)
 
-    for copy in (to_north, to_south, to_west, to_east):
+    for copy in (to_north, to_south, to_east):
         copy.wait_send()
+
+    @pl.when(jnp.logical_or(jnp.logical_not(main), jnp.logical_and(keeps, lon == 1)))
+    def _():
+        to_west.wait_send()
 
 
 def body(lat_count, tracers, zonal_wind, meridional_wind, cutoff):
@@ -612,6 +649,7 @@
             pltpu.VMEM((2, fields + 1, levels, LANES), f32),
             pltpu.VMEM((2, levels, LANES), f32),
             pltpu.VMEM((2, levels, LANES), f32),
+            pltpu.VMEM((levels, LANES), f32),
             pltpu.VMEM((6, 256, 256), bf16),
             pltpu.VMEM((6, 256, 256), bf16),
             pltpu.VMEM((6, 256, 256), bf16),
@@ -625,7 +663,8 @@
             pltpu.VMEM((SECTORS, 4, 8, LANES), f32),
             pltpu.VMEM((SECTORS, 4, 8, LANES), f32),
             pltpu.VMEM((tiles, 8, LANES), f32),
-            dma((3,)), dma((6,)), dma((4,)), dma((4,)), dma, dma, dma, dma((6,)), pltpu.SemaphoreType.REGULAR((SECTORS,)),
+            dma((3,)), dma((6,)), dma((4,)), dma((4,)), dma, dma, dma, dma((2,)), dma((6,)), pltpu.SemaphoreType.REGULAR((SECTORS,)),
+            pltpu.SemaphoreType.REGULAR,
             dma((2,)), dma((2,)), dma((2,)), dma((2,)),
         ],
         compiler_params=pltpu.CompilerParams(

time: 42.9 us -> 38.6 us (0.90)
  Pallas kernels: 40.9 us -> 36.7 us
    pallas_call x1, Pallas kernels: 40.9 us -> 36.7 us  [body(): pl.pallas_call(functools.partial(kernel, lat_count, fields, rows), out_sh...]
where the time goes in v8:
time: 38.6 us; the launch traced here: 38.4 us
  Pallas kernels  36.7 us (95%)
  local copies, waits for them, and re-layouts  1.75 us (5%)
    pallas_call x1, Pallas kernels, body(): pl.pallas_call(functools.partial(kernel, lat_count, fields, rows), out_sh...  36.7 us
    unnamed x1, local copies, waits for them, and re-layouts  1.75 us

profile of v8, /device:TPU:1, one launch (start us, length us, event | category | flops | bytes accessed | tf_op | source)
XLA Modules:
  0.0 38.4 jit_solution(2904949490722485216)
XLA Ops:
  0.0 36.7 %shard_map.91 = f32[5,9,16,120]{3,2,1,0:T(8,128)} custom-call(f32[5,9,16,120]{3,2,1,0:T(8,128)} %bitcast.5, f32[9,16,120]{2,1,0:T(8,128)} %bitcast.6, f32[9,16,120]{2,1,0:T(8,128)} %bitcast.7, s32[9]{0:T(128)} %cut_hbm.1, bf16[6,256,256]{2,1,0:T(8,128)(2,1)} %constant.10.clone.fh_hbm, bf16[6,256,256]{2,1,0:T(8,128)(2,1)} %constant.11.clone.fl_hbm, ...), custom_call_target="tpu_custom_call" | custom-call | tf_op jit(solution)/shard_map/pallas_call | solution.py:636
  36.7 1.7 %copy.11 = f32[5,16,9,120]{3,1,2,0:T(8,128)} copy(f32[5,16,9,120]{3,1,2,0:T(8,128)} %bitcast.4) | data formatting | bytes 691200

commit v9 on v8

--- a/solution.py
+++ b/solution.py
@@ -135,7 +135,9 @@
     x_high = x.astype(jnp.bfloat16)
     x_low = (x - x_high.astype(jnp.float32)).astype(jnp.bfloat16)
     dot = functools.partial(jnp.dot, preferred_element_type=jnp.float32)
-    return dot(x_high, high) + (dot(x_low, high) + dot(x_high, low))
+    count = x.shape[0]
+    both = dot(jnp.concatenate([x_high, x_low], axis=0), high)
+    return both[:count] + (both[count:] + dot(x_high, low))
 
 
 def kernel(
@@ -276,22 +278,12 @@
 
     sector = q_in.shape[-1]
     lane = lax.broadcasted_iota(jnp.int32, (16, LANES), 1)
-    east_pack = jnp.zeros((16, LANES), jnp.float32)
-    west_pack = jnp.zeros((16, LANES), jnp.float32)
-    for f in range(fields + 1):
+    for f in range(fields):
         for r in range(rows):
-            s = f * rows + r
-            source, pad = (q_in.at[f], q_pad.at[f]) if f < fields else (u_in, u_pad)
-            pad[r, :, pl.ds(0, sector)] = source[r]
-            x = pad[r]
-            west_pack = jnp.where(lane == s, pltpu.roll(x, s, 1), west_pack)
-            east_pack = jnp.where(
-                lane == s, pltpu.roll(x, (s - (sector - 1)) % LANES, 1), east_pack
-            )
+            q_pad[f, r, :, pl.ds(0, sector)] = q_in[f, r]
     for r in range(rows):
+        u_pad[r, :, pl.ds(0, sector)] = u_in[r]
         v_pad[r, :, pl.ds(0, sector)] = v_in[r]
-    side_out[0] = west_pack
-    side_out[1] = east_pack
     for side, row in ((0, 0), (1, rows - 1)):
         for f in range(fields):
             edge_out[side, f] = q_pad[f, row]
@@ -317,10 +309,24 @@
         src_ref=side_out.at[1], dst_ref=side_in.at[0], send_sem=halo_send.at[3],
         recv_sem=halo_recv.at[3], device_id=east, device_id_type=MESH,
     )
+    known = rank >= SECTORS // 2
     for copy, pole, late in ((to_north, low_edge, north_late), (to_south, high_edge, south_late)):
-        @pl.when(jnp.logical_not(jnp.logical_or(pole, late)))
+        @pl.when(jnp.where(pole, known, jnp.logical_not(late)))
         def _():
             copy.start()
+
+    east_pack = jnp.zeros((16, LANES), jnp.float32)
+    west_pack = jnp.zeros((16, LANES), jnp.float32)
+    for f in range(fields + 1):
+        for r in range(rows):
+            s = f * rows + r
+            x = q_pad[f, r] if f < fields else u_pad[r]
+            west_pack = jnp.where(lane == s, pltpu.roll(x, s, 1), west_pack)
+            east_pack = jnp.where(
+                lane == s, pltpu.roll(x, (s - (sector - 1)) % LANES, 1), east_pack
+            )
+    side_out[0] = west_pack
+    side_out[1] = east_pack
 
     @pl.when(jnp.logical_not(team_member))
     def _():
@@ -501,7 +507,7 @@
                         pl.semaphore_wait(hello.at[t], 1)
 
                     for copy, pole in ((to_north, low_edge), (to_south, high_edge)):
-                        @pl.when(jnp.logical_and(pole, to == across))
+                        @pl.when(jnp.logical_and(pole, jnp.logical_and(to == across, jnp.logical_not(known))))
                         def _():
                             copy.start()
 
@@ -573,12 +579,12 @@
                             back_send.at[phase], back_recv.at[phase], (team, to),
                         )
 
-                    for offset in OFFSETS:
-                        back(turned(offset))
-
-                    @pl.when(helper)
-                    def _():
-                        back(lon)
+                    for t in range(SECTORS):
+                        to = lax.rem(t + jnp.where(team == 0, 1, 0), SECTORS)
+
+                        @pl.when(jnp.logical_or(helper, to != lon))
+                        def _():
+                            back(to)
 
             @pl.when(main)
             def _():

time: 38.6 us -> 37.6 us (0.974)
  Pallas kernels: 36.7 us -> 35.7 us
    pallas_call x1, Pallas kernels: 36.7 us -> 35.7 us  [body(): pl.pallas_call(functools.partial(kernel, lat_count, fields, rows), out_sh...]
where the time goes in v9:
time: 37.6 us; the launch traced here: 37.4 us
  Pallas kernels  35.7 us (95%)
  local copies, waits for them, and re-layouts  1.75 us (5%)
    pallas_call x1, Pallas kernels, body(): pl.pallas_call(functools.partial(kernel, lat_count, fields, rows), out_sh...  35.7 us
    unnamed x1, local copies, waits for them, and re-layouts  1.75 us

profile of v9, /device:TPU:1, one launch (start us, length us, event | category | flops | bytes accessed | tf_op | source)
XLA Modules:
  0.0 37.4 jit_solution(6973737618770237979)
XLA Ops:
  0.0 35.7 %shard_map.91 = f32[5,9,16,120]{3,2,1,0:T(8,128)} custom-call(f32[5,9,16,120]{3,2,1,0:T(8,128)} %bitcast.5, f32[9,16,120]{2,1,0:T(8,128)} %bitcast.6, f32[9,16,120]{2,1,0:T(8,128)} %bitcast.7, s32[9]{0:T(128)} %cut_hbm.1, bf16[6,256,256]{2,1,0:T(8,128)(2,1)} %constant.10.clone.fh_hbm, bf16[6,256,256]{2,1,0:T(8,128)(2,1)} %constant.11.clone.fl_hbm, ...), custom_call_target="tpu_custom_call" | custom-call | tf_op jit(solution)/shard_map/pallas_call | solution.py:642
  35.7 1.7 %copy.11 = f32[5,16,9,120]{3,1,2,0:T(8,128)} copy(f32[5,16,9,120]{3,1,2,0:T(8,128)} %bitcast.4) | data formatting | bytes 691200

commit v10 on v9

--- a/solution.py
+++ b/solution.py
@@ -426,8 +426,9 @@
             stepped[2 * p] = new[:8]
             stepped[2 * p + 1] = new[8:]
 
-    def hand_out(source):
-        for p, (f, r) in enumerate(order):
+    def hand_out(source, places):
+        for p in places:
+            f, r = order[p]
             out_ref[f, r] = source[pl.ds(2 * p, 2)].reshape(16, LANES)[:, :sector]
 
     @pl.when(main)
@@ -593,8 +594,9 @@
     @pl.when(main)
     def _():
         waiter(result.at[pl.ds(0, 46)], back_recv.at[0]).wait()
+        hand_out(result, range(24))
         waiter(result.at[pl.ds(0, 40)], back_recv.at[1]).wait()
-        hand_out(result)
+        hand_out(result, range(24, 45))
         waiter(stepped.at[pl.ds(0, 22)], go_send.at[1]).wait()
         for phase in range(2):
             waiter(stepped.at[pl.ds(0, 22)], back_send.at[phase]).wait()
@@ -618,7 +620,7 @@
         set_ghosts(range(len(order)), True)
         edges_arrive()
         step(range(len(order)), {}, True)
-        hand_out(stepped)
+        hand_out(stepped, range(len(order)))
 
     for copy in (to_north, to_south, to_east):
         copy.wait_send()

time: 37.6 us -> 37.6 us (level)
  no operation moved by 1% of the time
where the time goes in v10:
time: 37.6 us; the launch traced here: 37.4 us
  Pallas kernels  35.7 us (95%)
  local copies, waits for them, and re-layouts  1.75 us (5%)
    pallas_call x1, Pallas kernels, body(): pl.pallas_call(functools.partial(kernel, lat_count, fields, rows), out_sh...  35.7 us
    unnamed x1, local copies, waits for them, and re-layouts  1.75 us

profile of v10, /device:TPU:1, one launch (start us, length us, event | category | flops | bytes accessed | tf_op | source)
XLA Modules:
  0.0 37.4 jit_solution(16890914636461039825)
XLA Ops:
  0.0 35.7 %shard_map.91 = f32[5,9,16,120]{3,2,1,0:T(8,128)} custom-call(f32[5,9,16,120]{3,2,1,0:T(8,128)} %bitcast.5, f32[9,16,120]{2,1,0:T(8,128)} %bitcast.6, f32[9,16,120]{2,1,0:T(8,128)} %bitcast.7, s32[9]{0:T(128)} %cut_hbm.1, bf16[6,256,256]{2,1,0:T(8,128)(2,1)} %constant.10.clone.fh_hbm, bf16[6,256,256]{2,1,0:T(8,128)(2,1)} %constant.11.clone.fl_hbm, ...), custom_call_target="tpu_custom_call" | custom-call | tf_op jit(solution)/shard_map/pallas_call | solution.py:644
  35.7 1.7 %copy.11 = f32[5,16,9,120]{3,1,2,0:T(8,128)} copy(f32[5,16,9,120]{3,1,2,0:T(8,128)} %bitcast.4) | data formatting | bytes 691200
